TPU v7x, 256 devices: a whole 4x4x8 slice. The times are simulated.
256 devices in a mesh: band: 32 (over y_hi, z, core), member: 8 (over y_lo, x).
Axes of the slice: x: 4, y: 4 (y_hi: 2, y_lo: 2; y = y_hi * 2 + y_lo), z: 8, core: 2. Of those that a mesh axis runs over, the one named last changes fastest.
Arguments:
- grid_latent: bfloat16 [8, 32768, 512], P('member', 'band'), may hold values from -6 to 6
- mesh_latent: bfloat16 [8, 32768, 512], P('member', 'band'), may hold values from -6 to 6
- edge_attr: bfloat16 [4, 4, 32768], P(None, None, 'band'), may hold values from -5 to 5
- neighbours: int32 [32768, 4], P('band'), may hold values from 0 to 2047, as said below
- send_rows: int32 [64, 512], P('band'), may hold values from 0 to 1023, as said below
- target: float32 [100, 32768], P(None, 'band'), may hold values from -6 to 6
- field_weight: float32 [100], replicated, may hold values from 1 to 10
- w_src: bfloat16 [512, 512], replicated, may hold values from -0.25 to 0.25
- w_dst: bfloat16 [512, 512], replicated, may hold values from -0.25 to 0.25
- w_edge: bfloat16 [4, 512], replicated, may hold values from -3 to 3
- w_msg: bfloat16 [512, 512], replicated, may hold values from -0.25 to 0.25
- ln_gain: float32 [512], replicated, may hold values from 0.1 to 1.9
- w_out: bfloat16 [512, 100], replicated, may hold values from -0.25 to 0.25
Outputs:
- d_grid: bfloat16 [8, 32768, 512], P('member', 'band')
- d_mesh: bfloat16 [8, 32768, 512], P('member', 'band')
Inputs may be any that keep to these rules, and one draw needn't show every extreme that they name: `neighbours`: grid points of band index 0 never name slots 1024 to 1535, those of the last band index never name slots 1024 + 512 and up. `send_rows`: the two lists of one band index hold 1024 distinct rows together.
All inputs are finite; a program needn't handle non-finite values.
Results may differ from a plain program's by a relative error of at most 0.04.
Values may be sent and summed in bfloat16 or wider, within the bound.
A program may use at most 128 MiB of HBM per device.

v0:
```python
import jax
import jax.numpy as jnp
from jax import lax
from jax.sharding import PartitionSpec as P

DELTA_SQ = 0.0625
ALPHA = 0.95
LN_EPS = 1e-05


def extended(block, sides, width):
    for axis, dim in sides:
        count = lax.axis_size(axis)
        forward = [(i, i + 1) for i in range(count - 1)]
        backward = [(target, source) for source, target in forward]
        low = lax.ppermute(
            lax.slice_in_dim(block, block.shape[dim] - width, None, axis=dim), axis, forward
        )
        high = lax.ppermute(lax.slice_in_dim(block, 0, width, axis=dim), axis, backward)
        block = jnp.concatenate([low, block, high], axis=dim)
    return block


def slope(diff):
    return diff / jnp.sqrt(diff * diff + DELTA_SQ)


def times_transposed(left, weight):
    return lax.dot_general(
        left, weight, (((1,), (1,)), ((), ())), preferred_element_type=jnp.float32
    )


def per_device(
    grid_latent,
    mesh_latent,
    edge_attr,
    neighbours,
    send_rows,
    target,
    field_weight,
    w_src,
    w_dst,
    w_edge,
    w_msg,
    ln_gain,
    w_out,
):
    grid_rows = grid_latent[0]
    mesh_rows = mesh_latent[0]
    points = grid_rows.shape[0]
    channels = grid_rows.shape[1]
    owned = mesh_rows.shape[0]
    halo_rows = send_rows.shape[1]
    edges = neighbours.shape[1]
    framed = extended(mesh_rows[send_rows], (("band", 0),), 1)
    slot_rows = jnp.concatenate([mesh_rows, framed[0], framed[3]], axis=0)
    src_slots = jnp.dot(slot_rows, w_src, preferred_element_type=jnp.float32).astype(jnp.bfloat16)
    dst = jnp.dot(grid_rows, w_dst, preferred_element_type=jnp.float32)
    edge_embed = jnp.einsum(
        "ekg,eh->gkh",
        edge_attr.astype(jnp.float32),
        w_edge.astype(jnp.float32),
        preferred_element_type=jnp.float32,
    )
    pre = src_slots[neighbours].astype(jnp.float32) + dst[:, None, :] + edge_embed
    act = jax.nn.silu(pre).astype(jnp.bfloat16)
    agg = jnp.dot(act.reshape(points * edges, channels), w_msg, preferred_element_type=jnp.float32)
    z_rows = grid_rows.astype(jnp.float32) + agg.reshape(points, edges, channels).sum(axis=1)
    centre = z_rows - jnp.mean(z_rows, axis=1, keepdims=True)
    rstd = 1.0 / jnp.sqrt(jnp.mean(centre * centre, axis=1, keepdims=True) + LN_EPS)
    zhat = centre * rstd
    normed = (zhat * ln_gain[None, :]).astype(jnp.bfloat16)
    pred = lax.dot_general(
        w_out, normed, (((0,), (1,)), ((), ())), preferred_element_type=jnp.float32
    )
    count = lax.axis_size("member")
    coeff = ALPHA / (count - 1) + (1.0 - ALPHA) / count
    ensemble = lax.all_gather(pred[None].astype(jnp.bfloat16), "member", axis=0, tiled=True).astype(
        jnp.float32
    )
    spread = jnp.sum(slope(pred[None] - ensemble), axis=0)
    d_pred = (field_weight[:, None] * (slope(pred - target) - coeff * spread)).astype(jnp.bfloat16)
    d_u = lax.dot_general(
        d_pred, w_out, (((0,), (1,)), ((), ())), preferred_element_type=jnp.float32
    )
    scaled = d_u * ln_gain[None, :]
    d_z = rstd * (
        scaled
        - jnp.mean(scaled, axis=1, keepdims=True)
        - zhat * jnp.mean(scaled * zhat, axis=1, keepdims=True)
    )
    d_act = times_transposed(d_z.astype(jnp.bfloat16), w_msg)
    sigma = jax.nn.sigmoid(pre)
    d_pre = (d_act[:, None, :] * (sigma * (1.0 + pre * (1.0 - sigma)))).astype(jnp.bfloat16)
    d_sum = jnp.sum(d_pre.astype(jnp.float32), axis=1).astype(jnp.bfloat16)
    d_grid = (d_z + times_transposed(d_sum, w_dst)).astype(jnp.bfloat16)
    total_slots = owned + 2 * halo_rows
    slot_grad = jax.ops.segment_sum(
        d_pre.reshape(points * edges, channels).astype(jnp.float32),
        neighbours.reshape(-1),
        num_segments=total_slots,
    )
    slot_grad = slot_grad.astype(jnp.bfloat16)
    targets_rows = jnp.concatenate([send_rows[0], send_rows[1]], axis=0)
    contrib = times_transposed(slot_grad, w_src)
    rims = jnp.stack([contrib[owned : owned + halo_rows], contrib[owned + halo_rows :]], axis=0)
    back = extended(rims.astype(jnp.bfloat16), (("band", 0),), 1).astype(rims.dtype)
    returned = jnp.concatenate([back[0], back[3]], axis=0)
    d_mesh = contrib[:owned] + jax.ops.segment_sum(returned, targets_rows, num_segments=owned)
    return (d_grid[None], d_mesh.astype(jnp.bfloat16)[None])


def solution(mesh):
    placed = (
        P("member", "band", None),
        P("member", "band", None),
        P(None, None, "band"),
        P("band", None),
        P("band", None),
        P(None, "band"),
        P(),
        P(),
        P(),
        P(),
        P(),
        P(),
        P(),
    )
    return jax.shard_map(
        per_device,
        mesh=mesh,
        in_specs=placed,
        out_specs=(P("member", "band", None), P("member", "band", None)),
        check_vma=False,
    )
```

profile of v0, /device:TPU:24, one launch (start us, length us, event | category | flops | bytes accessed | tf_op | source)
XLA Modules:
  0.0 231.1 jit_solution(4873283581345426935)
XLA Ops:
  7.2 0.0 copy-start
  7.2 0.0 all-gather.4.cloned.1.call-start
  7.2 0.7 fusion.34
  8.0 5.3 %gather_fusion = bf16[1024,512]{1,0:T(8,128)(2,1)S(1)} fusion(bf16[1024,512]{1,0:T(8,128)(2,1)} %bitcast.50, s32[1024]{0:T(1024)S(1)} %broadcast_clamp_fusion.1), kind=kCustom, calls=%fused_computation | custom fusion | bytes 2101248 | tf_op jit(solution)/shard_map/gather | solution.py:56
  13.3 0.0 copy-start.15
  13.3 0.0 copy-start.6
  13.4 0.9 slice_bitcast_fusion.3
  14.2 8.0 %collective-permute-start.1 = (bf16[1,512,512]{2,1,0:T(8,128)(2,1)}, bf16[1,512,512]{2,1,0:T(8,128)(2,1)}, u32[]{:S(2)}, u32[]{:S(2)}) collective-permute-start(bf16[1,512,512]{2,1,0:T(8,128)(2,1)} %get-tuple-element.19), channel_id=1, source_target_pairs={{8,0},{16,8},{24,16},{32,24},{40,32},{48,40},{56,48},{64,56},{72,6... | collective-permute-start | bytes 1572872 | tf_op jit(solution)/shard_map/ppermute | solution.py:19
  22.2 1.9 collective-permute-start
  24.2 0.2 copy.34
  24.4 0.3 reshape.49
  24.7 0.0 copy-done.6
  24.7 1.3 copy.33
  26.0 0.0 copy-done.10
  26.0 2.1 fusion.21
  28.1 1.1 collective-permute-done.1
  29.2 7.2 %collective-permute-done = bf16[1,512,512]{2,1,0:T(8,128)(2,1)} collective-permute-done((bf16[1,512,512]{2,1,0:T(8,128)(2,1)S(1)}, bf16[1,512,512]{2,1,0:T(8,128)(2,1)}, u32[]{:S(2)}, u32[]{:S(2)}) %collective-permute-start) | collective-permute-done | bytes 524320 | tf_op jit(solution)/shard_map/ppermute | solution.py:16
  36.5 2.4 %convolution_convert_fusion = bf16[2048,512]{1,0:T(8,128)(2,1)S(1)} fusion(bf16[512,512]{1,0:T(8,128)(2,1)S(1)} %copy-done, bf16[512,512]{1,0:T(8,128)(2,1)} %bitcast.5, bf16[512,512]{1,0:T(8,128)(2,1)} %bitcast.3, bf16[1024,512]{1,0:T(8,128)(2,1)S(1)} %bitcast.51), kind=kOutput, calls=%fused_computation.15 | convolution fusion | flops 1081081856 | bytes 4718592 | tf_op jit(solution)/shard_map/dot_general | solution.py:58
  38.9 17.4 %gather_fusion.1 = bf16[4096,512]{1,0:T(8,128)(2,1)} fusion(bf16[2048,512]{1,0:T(8,128)(2,1)S(1)} %convolution_convert_fusion, s32[4096]{0:T(1024)S(1)} %broadcast_clamp_fusion), kind=kCustom, calls=%fused_computation.1 | custom fusion | bytes 8404992 | tf_op jit(solution)/shard_map/gather | solution.py:66
  56.3 8.3 %reshape.81 = f32[1024,4,512]{2,1,0:T(4,128)} reshape(bf16[4096,512]{1,0:T(8,128)(2,1)} %gather_fusion.1) | data formatting | bytes 12582912 | tf_op jit(solution)/shard_map/convert_element_type | solution.py:66
  64.6 10.1 %copy.36 = f32[1024,4,512]{0,2,1:T(8,128)} copy(f32[1024,4,512]{2,1,0:T(4,128)} %reshape.81) | data formatting | bytes 16777216 | tf_op jit(solution)/shard_map/convert_element_type | solution.py:66
  74.7 0.0 copy-done.16
  74.7 0.0 copy-start.8
  74.7 4.7 %bitcast_add_fusion = f32[1024,4,512]{0,2,1:T(8,128)S(1)} fusion(f32[1024,4,512]{0,2,1:T(8,128)} %copy.36, f32[1024,512]{0,1:T(8,128)S(1)} %copy-done.5, bf16[4,4,1024]{2,1,0:T(4,128)(2,1)S(1)} %copy-done.16, bf16[4,512]{1,0:T(4,128)(2,1)S(1)} %copy-done.19), kind=kOutput, calls=%fused_computation.4 | convolution fusion | flops 20971520 | bytes 18911232 | tf_op jit(solution)/shard_map/ekg,eh->gkh/dot_general | solution.py:60
  79.5 3.2 %copy-done.2 = f32[1024,4,512]{0,2,1:T(8,128)} copy-done((f32[1024,4,512]{0,2,1:T(8,128)}, f32[1024,4,512]{0,2,1:T(8,128)S(1)}, u32[]{:S(2)}) %copy-start.2) | copy-done | bytes 8388632
  82.7 2.8 %fusion.6 = f32[1024,512]{1,0:T(8,128)S(1)} fusion(f32[1024,4,512]{0,2,1:T(8,128)S(1)} %bitcast_add_fusion, bf16[512,512]{1,0:T(8,128)(2,1)S(1)} %copy-done.8), kind=kOutput, calls=%fused_computation.16 | convolution fusion | flops 2159542272 | bytes 11010048 | tf_op jit(solution)/shard_map/dot_general | solution.py:68
  85.5 1.9 copy.39
  87.4 2.2 fusion.41
  89.6 0.0 copy-start.13
  89.6 0.0 copy-start.17
  89.7 0.3 multiply_reduce_fusion.1
  90.0 0.6 copy-done.13
  90.5 0.4 convolution_bitcast_fusion
  91.0 0.0 copy-start.12
  91.0 0.0 copy-start.20
  91.0 0.7 convert_bitcast_fusion.3
  91.7 0.0 all-gather.4.cloned.1.call-update
  91.7 1.0 copy.42
  92.8 1.3 reshape.57
  94.1 36.4 %all-gather.4.cloned.1.call-done = bf16[8,100,1024]{2,1,0:T(8,128)(2,1)} async-done(((bf16[1,100,1024]{2,1,0:T(8,128)(2,1)}), bf16[8,100,1024]{2,1,0:T(8,128)(2,1)}) %all-gather.4.cloned.1.call-update) | async-done | bytes 1638416 | tf_op jit(solution)/shard_map/all_gather | solution.py:79
  130.4 2.3 %fusion.5 = f32[100,1024]{1,0:T(8,128)S(1)} fusion(bf16[8,100,1024]{2,1,0:T(8,128)(2,1)} %all-gather.4.cloned.1.call-done, f32[100,1024]{1,0:T(8,128)S(1)} %convolution_bitcast_fusion), kind=kLoop, calls=%fused_computation.14 | loop fusion | flops 4812800 | bytes 2457600 | tf_op jit(solution)/shard_map/reduce_sum | solution.py:82
  132.8 0.0 copy-start.9
  132.8 0.7 multiply_reduce_fusion.2
  133.6 1.3 copy-done.3
  134.9 0.9 fusion.23
  135.8 8.0 %fusion.40 = (bf16[1024,512]{0,1:T(8,128)(2,1)}, bf16[1024,4,512]{0,2,1:T(8,128)(2,1)}) fusion(f32[1024,4,512]{0,2,1:T(8,128)} %copy-done.2, f32[1024,512]{0,1:T(8,128)S(1)} %fusion.23), kind=kLoop, calls=%fused_computation.80 | loop fusion | flops 20447232 | bytes 15728640 | tf_op jit(solution)/shard_map/reduce_sum | solution.py:96
  143.8 8.4 %copy.43 = f32[1024,4,512]{2,1,0:T(4,128)} copy(bf16[1024,4,512]{0,2,1:T(8,128)(2,1)} %get-tuple-element.11) | data formatting | bytes 12582912 | tf_op jit(solution)/shard_map/convert_element_type | solution.py:100
  152.2 10.0 %reshape.59 = f32[4096,512]{1,0:T(8,128)} reshape(f32[1024,4,512]{2,1,0:T(4,128)} %copy.43) | data formatting | bytes 16777216 | tf_op jit(solution)/shard_map/convert_element_type | solution.py:100
  162.2 27.4 %scatter_custom_fusion = f32[2048,512]{1,0:T(8,128)} fusion(s32[4096]{0:T(1024)S(1)} %reshape.57, f32[4096,512]{1,0:T(8,128)} %reshape.59, f32[]{:T(128)} %constant.14.clone.1), kind=kCustom, calls=%fused_computation.28 | custom fusion | flops 2097152 | bytes 4194816 | tf_op jit(solution)/shard_map/scatter-add | solution.py:99
  189.6 5.5 %fusion.43 = (bf16[2048,512]{1,0:T(8,128)(2,1)S(1)}, f32[2048,512]{1,0:T(8,128)}) fusion(bf16[512,512]{1,0:T(8,128)(2,1)S(1)} %copy-done, f32[2048,512]{1,0:T(8,128)} %scatter_custom_fusion), kind=kOutput, calls=%fused_computation.83 | convolution fusion | flops 1075838976 | bytes 11010048 | tf_op jit(solution)/shard_map/dot_general | solution.py:29
  195.1 0.9 slice_bitcast_fusion.1
  196.0 1.9 collective-permute-start.3
  197.9 2.4 %collective-permute-start.2 = (bf16[1,512,512]{2,1,0:T(8,128)(2,1)S(1)}, bf16[1,512,512]{2,1,0:T(8,128)(2,1)}, u32[]{:S(2)}, u32[]{:S(2)}) collective-permute-start(bf16[1,512,512]{2,1,0:T(8,128)(2,1)S(1)} %get-tuple-element.16), channel_id=1, source_target_pairs={{0,8},{8,16},{16,24},{24,32},{32,40},{40,48},{48,56},{56,64},{64,7... | collective-permute-start | bytes 1572872 | tf_op jit(solution)/shard_map/ppermute | solution.py:16
  200.4 0.0 copy-done.7
  200.4 0.0 copy-done.11
  200.4 0.0 copy-done.4
  200.4 2.0 fusion.20
  202.4 2.3 copy.44
  204.7 1.8 slice.48
  206.4 0.0 collective-permute-done.3
  206.4 5.7 %collective-permute-done.2 = bf16[1,512,512]{2,1,0:T(8,128)(2,1)} collective-permute-done((bf16[1,512,512]{2,1,0:T(8,128)(2,1)S(1)}, bf16[1,512,512]{2,1,0:T(8,128)(2,1)}, u32[]{:S(2)}, u32[]{:S(2)}) %collective-permute-start.2) | collective-permute-done | bytes 524320 | tf_op jit(solution)/shard_map/ppermute | solution.py:16
  212.1 2.7 %convert_bitcast_fusion = (f32[512,512]{1,0:T(8,128)}, f32[512,512]{1,0:T(8,128)}) fusion(bf16[1,512,512]{2,1,0:T(8,128)(2,1)} %collective-permute-done.3, bf16[1,512,512]{2,1,0:T(8,128)(2,1)S(1)} %get-tuple-element.16, bf16[1,512,512]{2,1,0:T(8,128)(2,1)} %get-tuple-element.17, bf16[1,512,512]{2,1,0:T(8,128)(2,1)} %collective-permute-done.2), kind=kLoop, calls=%fused_computation.40 | loop fusion | flops 2097152 | bytes 4194304 | tf_op jit(solution)/shard_map/squeeze | solution.py:109
  214.8 8.3 %scatter_custom_fusion.1 = f32[1024,512]{1,0:T(8,128)S(1)} fusion(f32[1024,512]{1,0:T(8,128)S(1)} %slice.48, s32[1024]{0:T(1024)S(1)} %pad_add_fusion, f32[512,512]{1,0:T(8,128)} %get-tuple-element.15, f32[]{:T(128)} %constant.34, f32[512,512]{1,0:T(8,128)} %get-tuple-element.14), kind=kCustom, calls=%fused_computation.22 | custom fusion | flops 1048576 | bytes 4194308 | tf_op jit(solution)/shard_map/scatter-add | solution.py:110
  223.1 1.1 convert_bitcast_fusion.1
  (33 shorter events, 0.1 us)
Async XLA Ops:
  7.2 29.3 %copy-start = (bf16[512,512]{1,0:T(8,128)(2,1)S(1)}, bf16[512,512]{1,0:T(8,128)(2,1)}, u32[]{:S(2)}) copy-start(bf16[512,512]{1,0:T(8,128)(2,1)} %param.20) | copy-start | bytes 1572868
  7.2 123.3 %all-gather.4.cloned.1.call-start = ((), (), s32[]{:S(2)}) async-start(), calls=%async_computation | async-start | bytes 1916928 | tf_op jit(solution)/shard_map/all_gather | solution.py:79
  13.3 10.8 %copy-start.15 = (s32[1024,4]{0,1:T(4,128)S(1)}, s32[1024,4]{0,1:T(4,128)}, u32[]{:S(2)}) copy-start(s32[1024,4]{0,1:T(4,128)} %param.16) | copy-start | bytes 49156
  13.3 11.3 %copy-start.6 = (bf16[1,1024,512]{2,1,0:T(8,128)(2,1)S(1)}, bf16[1,1024,512]{2,1,0:T(8,128)(2,1)}, u32[]{:S(2)}) copy-start(bf16[1,1024,512]{2,1,0:T(8,128)(2,1)} %param.13) | copy-start | bytes 3145732
  14.2 11.8 %copy-start.10 = (bf16[512,512]{1,0:T(8,128)(2,1)S(1)}, bf16[512,512]{1,0:T(8,128)(2,1)}, u32[]{:S(2)}) copy-start(bf16[512,512]{1,0:T(8,128)(2,1)} %param.21) | copy-start | bytes 1572868
  14.2 15.0 %collective-permute-start.1 = (bf16[1,512,512]{2,1,0:T(8,128)(2,1)}, bf16[1,512,512]{2,1,0:T(8,128)(2,1)}, u32[]{:S(2)}, u32[]{:S(2)}) collective-permute-start(bf16[1,512,512]{2,1,0:T(8,128)(2,1)} %get-tuple-element.19), channel_id=1, source_target_pairs={{8,0},{16,8},{24,16},{32,24},{40,32},{48,40},{56,48},{64,56},{72,6... | collective-permute-start | bytes 1572872 | tf_op jit(solution)/shard_map/ppermute | solution.py:19
  22.2 14.2 %collective-permute-start = (bf16[1,512,512]{2,1,0:T(8,128)(2,1)S(1)}, bf16[1,512,512]{2,1,0:T(8,128)(2,1)}, u32[]{:S(2)}, u32[]{:S(2)}) collective-permute-start(bf16[1,512,512]{2,1,0:T(8,128)(2,1)S(1)} %get-tuple-element.18), channel_id=1, source_target_pairs={{0,8},{8,16},{16,24},{24,32},{32,40},{40,48},{48,56},{56,64},{64,7... | collective-permute-start | bytes 1572872 | tf_op jit(solution)/shard_map/ppermute | solution.py:16
  26.0 10.4 %copy-start.1 = (bf16[1,1024,512]{2,1,0:T(8,128)(2,1)S(1)}, bf16[1,1024,512]{2,1,0:T(8,128)(2,1)}, u32[]{:S(2)}) copy-start(bf16[1,1024,512]{2,1,0:T(8,128)(2,1)} %param.14) | copy-start | bytes 3145732
  64.6 10.1 %copy-start.5 = (f32[1024,512]{0,1:T(8,128)S(1)}, f32[1024,512]{0,1:T(8,128)}, u32[]{:S(2)}) copy-start(f32[1024,512]{0,1:T(8,128)} %fusion.21) | copy-start | bytes 6291460
  64.6 10.1 %copy-start.16 = (bf16[4,4,1024]{2,1,0:T(4,128)(2,1)S(1)}, bf16[4,4,1024]{2,1,0:T(4,128)(2,1)}, u32[]{:S(2)}) copy-start(bf16[4,4,1024]{2,1,0:T(4,128)(2,1)} %param.15) | copy-start | bytes 98308
  64.6 10.1 %copy-start.19 = (bf16[4,512]{1,0:T(4,128)(2,1)S(1)}, bf16[4,512]{1,0:T(4,128)(2,1)}, u32[]{:S(2)}) copy-start(bf16[4,512]{1,0:T(4,128)(2,1)} %param.22) | copy-start | bytes 12292
  74.7 8.0 %copy-start.8 = (bf16[512,512]{1,0:T(8,128)(2,1)S(1)}, bf16[512,512]{1,0:T(8,128)(2,1)}, u32[]{:S(2)}) copy-start(bf16[512,512]{1,0:T(8,128)(2,1)} %param.23) | copy-start | bytes 1572868
  79.5 3.2 %copy-start.2 = (f32[1024,4,512]{0,2,1:T(8,128)}, f32[1024,4,512]{0,2,1:T(8,128)S(1)}, u32[]{:S(2)}) copy-start(f32[1024,4,512]{0,2,1:T(8,128)S(1)} %bitcast_add_fusion) | copy-start | bytes 25165828
  89.6 0.9 copy-start.13
  89.6 0.9 copy-start.17
  90.5 3.5 %copy-start.18 = (s32[2,512]{1,0:T(2,128)S(1)}, s32[2,512]{1,0:T(2,128)}, u32[]{:S(2)}) copy-start(s32[2,512]{1,0:T(2,128)} %param.17) | copy-start | bytes 12292
  91.0 41.8 %copy-start.12 = (f32[100,1024]{1,0:T(8,128)S(1)}, f32[100,1024]{1,0:T(8,128)}, u32[]{:S(2)}) copy-start(f32[100,1024]{1,0:T(8,128)} %param.18) | copy-start | bytes 1228804
  91.0 41.8 %copy-start.20 = (f32[100]{0:T(128)S(1)}, f32[100]{0:T(128)}, u32[]{:S(2)}) copy-start(f32[100]{0:T(128)} %param.19) | copy-start | bytes 1204
  130.4 2.3 %copy-start.14 = (bf16[512,100]{0,1:T(8,128)(2,1)S(1)}, bf16[512,100]{0,1:T(8,128)(2,1)}, u32[]{:S(2)}) copy-start(bf16[512,100]{0,1:T(8,128)(2,1)} %param.25) | copy-start | bytes 307204
  132.8 2.1 copy-start.9
  133.5 1.3 copy-start.3
  189.6 10.8 %copy-start.7 = (bf16[1024,512]{0,1:T(8,128)(2,1)S(1)}, bf16[1024,512]{0,1:T(8,128)(2,1)}, u32[]{:S(2)}) copy-start(bf16[1024,512]{0,1:T(8,128)(2,1)} %get-tuple-element.10) | copy-start | bytes 3145732
  189.6 10.8 %copy-start.11 = (bf16[512,512]{1,0:T(8,128)(2,1)S(1)}, bf16[512,512]{1,0:T(8,128)(2,1)}, u32[]{:S(2)}) copy-start(bf16[512,512]{1,0:T(8,128)(2,1)} %param.21) | copy-start | bytes 1572868
  195.1 5.2 %copy-start.4 = (f32[1024,512]{0,1:T(8,128)S(1)}, f32[1024,512]{0,1:T(8,128)}, u32[]{:S(2)}) copy-start(f32[1024,512]{0,1:T(8,128)} %copy-done.3) | copy-start | bytes 6291460
  196.0 10.4 %collective-permute-start.3 = (bf16[1,512,512]{2,1,0:T(8,128)(2,1)}, bf16[1,512,512]{2,1,0:T(8,128)(2,1)}, u32[]{:S(2)}, u32[]{:S(2)}) collective-permute-start(bf16[1,512,512]{2,1,0:T(8,128)(2,1)} %get-tuple-element.17), channel_id=1, source_target_pairs={{8,0},{16,8},{24,16},{32,24},{40,32},{48,40},{56,48},{64,56},{72,6... | collective-permute-start | bytes 1572872 | tf_op jit(solution)/shard_map/ppermute | solution.py:19
  197.9 14.2 %collective-permute-start.2 = (bf16[1,512,512]{2,1,0:T(8,128)(2,1)S(1)}, bf16[1,512,512]{2,1,0:T(8,128)(2,1)}, u32[]{:S(2)}, u32[]{:S(2)}) collective-permute-start(bf16[1,512,512]{2,1,0:T(8,128)(2,1)S(1)} %get-tuple-element.16), channel_id=1, source_target_pairs={{0,8},{8,16},{16,24},{24,32},{32,40},{40,48},{48,56},{56,64},{64,7... | collective-permute-start | bytes 1572872 | tf_op jit(solution)/shard_map/ppermute | solution.py:16
Sparse Core Ops, SparseCore 0:
  91.9 38.5 all-gather.3
where the time goes:
time: 233 us; the launch traced here: 231 us
  local copies, waits for them, and re-layouts  76.5 us (33%)
  other arithmetic  53.8 us (23%)
  waiting for transfers between devices  50.4 us (22%)
  matrix products  21.7 us (9%)
  between operations  14.4 us (6%)
  starting transfers between devices  14.3 us (6%)
    all_gather x1, waiting for transfers between devices, per_device(): lax.all_gather(pred[None].astype(jnp.bfloat16), 'member', axis=0, tiled=T...  36.4 us
    scatter-add x1, other arithmetic, per_device(): jax.ops.segment_sum(d_pre.reshape(points * edges, channels).astype(jnp.fl...  27.4 us
    convert_element_type x2, local copies, waits for them, and re-layouts, per_device(): src_slots[neighbours].astype(jnp.float32) + dst[:, None, :] + edge_embed  18.4 us
    convert_element_type x2, local copies, waits for them, and re-layouts, per_device(): d_pre.reshape(points * edges, channels).astype(jnp.float32)  18.4 us
    gather x1, local copies, waits for them, and re-layouts, per_device(): src_slots[neighbours].astype(jnp.float32) + dst[:, None, :] + edge_embed  17.4 us
    ppermute x2, waiting for transfers between devices, extended(): lax.ppermute(lax.slice_in_dim(block, block.shape[dim] - width, None, axis...  12.9 us
    ppermute x2, starting transfers between devices, extended(): lax.ppermute(lax.slice_in_dim(block, 0, width, axis=dim), axis, backward)  9.91 us
    unnamed x46, local copies, waits for them, and re-layouts  9.8 us
  transfers between devices with their start and end apart: 5, of which 4 were waited for; matrix products, arithmetic and copies ran while one was open for 5% of the time, Pallas kernels for 0%

commit v1 on v0

v1 whole, which is shorter than its diff:
```python
import functools

import jax
import jax.numpy as jnp
from jax import lax
from jax.experimental import pallas as pl
from jax.experimental.pallas import tpu as pltpu
from jax.sharding import PartitionSpec as P

DELTA_SQ = 0.0625
ALPHA = 0.95
LN_EPS = 1e-05

BF = jnp.bfloat16
F32 = jnp.float32
LANES = 128
CHUNKS = 4
MESH_ID = pl.DeviceIdType.MESH

COL_NEIGHBOUR = 100
COL_EDGE = 104
COL_SEND = 120


def dot(left, right):
    return jnp.dot(left, right, preferred_element_type=F32)


def dot_t(left, right):
    return lax.dot_general(left, right, (((1,), (1,)), ((), ())), preferred_element_type=F32)


def slope(diff):
    return diff * lax.rsqrt(diff * diff + DELTA_SQ)


def one_hot_columns(column, width):
    rows = column.shape[0]
    return jnp.where(lax.broadcasted_iota(jnp.int32, (rows, width), 1) == column, 1.0, 0.0).astype(BF)


def one_hot_rows(row, height, first):
    width = row.shape[1]
    return jnp.where(
        lax.broadcasted_iota(jnp.int32, (height, width), 0) + first == row, 1.0, 0.0
    ).astype(BF)


def kernel(
    n_band,
    n_member,
    grid_ref,
    mesh_ref,
    edge_ref,
    near_ref,
    send_ref,
    target_ref,
    weight_ref,
    w_src_ref,
    w_dst_ref,
    w_edge_ref,
    w_msg_ref,
    gain_ref,
    w_out_ref,
    d_grid_ref,
    d_mesh_ref,
    wide,
    table,
    w_out,
    src,
    out_halo,
    halo,
    own,
    deriv,
    zhat,
    rstd,
    pred,
    peers,
    d_peers,
    d_pred,
    d_halo,
    back,
    halo_send,
    halo_recv,
    pred_send,
    pred_recv,
    d_send,
    d_recv,
    back_send,
    back_recv,
):
    points, channels = grid_ref.shape
    owned = mesh_ref.shape[0]
    edges = near_ref.shape[0]
    rim = send_ref.shape[1]
    fields = target_ref.shape[0]
    chunk = points // CHUNKS
    share = chunk // n_member
    band = lax.axis_index("band")
    me = lax.axis_index("member")
    coeff = ALPHA / (n_member - 1) + (1.0 - ALPHA) / n_member

    barrier = pltpu.get_barrier_semaphore()
    for step in range(1, n_member):
        pl.semaphore_signal(
            barrier, inc=1, device_id={"member": lax.rem(me + step, n_member)}, device_id_type=MESH_ID
        )

    @pl.when(band > 0)
    def _():
        pl.semaphore_signal(barrier, inc=1, device_id={"band": band - 1}, device_id_type=MESH_ID)

    @pl.when(band < n_band - 1)
    def _():
        pl.semaphore_signal(barrier, inc=1, device_id={"band": band + 1}, device_id_type=MESH_ID)

    wide[...] = jnp.zeros_like(wide)
    wide[0:fields, :] = target_ref[...]
    wide[COL_NEIGHBOUR : COL_NEIGHBOUR + edges, :] = near_ref[...].astype(F32)
    for feature in range(edge_ref.shape[0]):
        wide[COL_EDGE + feature * edges : COL_EDGE + (feature + 1) * edges, :] = edge_ref[feature].astype(F32)
    wide[COL_SEND : COL_SEND + 1, 0:rim] = send_ref[0:1, :].astype(F32)
    wide[COL_SEND : COL_SEND + 1, rim : 2 * rim] = send_ref[1:2, :].astype(F32)
    table[...] = wide[...].T
    w_out[...] = jnp.zeros_like(w_out)
    w_out[0:fields, :] = w_out_ref[...]
    halo[2 * rim :, :] = jnp.zeros((LANES, channels), BF)
    for feature in range(edge_ref.shape[0]):
        for edge in range(edges):
            row = 2 * rim + COL_EDGE + feature * edges + edge
            halo[row : row + 1, :] = w_edge_ref[feature : feature + 1, :]

    src[...] = dot(mesh_ref[...], w_src_ref[...]).astype(BF)
    for side in range(2):
        column = table[side * rim : (side + 1) * rim, COL_SEND : COL_SEND + 1].astype(jnp.int32)
        out_halo[side] = dot(one_hot_columns(column, owned), src[...]).astype(BF)

    links = 0
    for step in range(1, n_member):
        links += 1
    pl.semaphore_wait(
        barrier, links + jnp.where(band > 0, 1, 0) + jnp.where(band < n_band - 1, 1, 0)
    )

    down = pltpu.make_async_remote_copy(
        src_ref=out_halo.at[0],
        dst_ref=halo.at[pl.ds(rim, rim)],
        send_sem=halo_send.at[0],
        recv_sem=halo_recv.at[1],
        device_id={"band": jnp.maximum(band - 1, 0)},
        device_id_type=MESH_ID,
    )
    up = pltpu.make_async_remote_copy(
        src_ref=out_halo.at[1],
        dst_ref=halo.at[pl.ds(0, rim)],
        send_sem=halo_send.at[1],
        recv_sem=halo_recv.at[0],
        device_id={"band": jnp.minimum(band + 1, n_band - 1)},
        device_id_type=MESH_ID,
    )
    has_below = band > 0
    has_above = band < n_band - 1

    @pl.when(has_below)
    def _():
        down.start()

    @pl.when(has_above)
    def _():
        up.start()

    @pl.when(jnp.logical_not(has_below))
    def _():
        halo[0:rim, :] = jnp.zeros((rim, channels), BF)
        back[0:rim, :] = jnp.zeros((rim, channels), BF)

    @pl.when(jnp.logical_not(has_above))
    def _():
        halo[rim : 2 * rim, :] = jnp.zeros((rim, channels), BF)
        back[rim : 2 * rim, :] = jnp.zeros((rim, channels), BF)

    def gather_own(part, _):
        first = pl.multiple_of(part * chunk, chunk)
        hot = jnp.concatenate(
            [
                one_hot_columns(
                    table[pl.ds(first, chunk), COL_NEIGHBOUR + edge : COL_NEIGHBOUR + edge + 1].astype(
                        jnp.int32
                    ),
                    owned,
                )
                for edge in range(edges)
            ],
            axis=0,
        )
        rows = dot(hot, src[...]).astype(BF)
        for edge in range(edges):
            own[edge, pl.ds(first, chunk), :] = rows[edge * chunk : (edge + 1) * chunk, :]
        return 0

    lax.fori_loop(0, CHUNKS, gather_own, 0)

    @pl.when(has_above)
    def _():
        down.wait_recv()

    @pl.when(has_below)
    def _():
        up.wait_recv()

    gain = gain_ref[...]

    def forward(part):
        rows = pl.ds(part * chunk, chunk)
        lane = lax.broadcasted_iota(jnp.int32, (chunk, LANES), 1)
        features = table[rows, :]
        hots = []
        for edge in range(edges):
            column = table[rows, COL_NEIGHBOUR + edge : COL_NEIGHBOUR + edge + 1].astype(jnp.int32)
            chosen = (lane >= COL_EDGE) & (lane < COL_SEND) & (lax.rem(lane, edges) == edge)
            hots.append(
                jnp.concatenate(
                    [
                        one_hot_columns(column - owned, 2 * rim),
                        jnp.where(chosen, features, 0.0).astype(BF),
                    ],
                    axis=1,
                )
            )
        read = dot(jnp.concatenate(hots, axis=0), halo[...])
        dst = dot(grid_ref[rows, :], w_dst_ref[...])
        total = None
        for edge in range(edges):
            pre = read[edge * chunk : (edge + 1) * chunk, :] + own[edge, rows, :].astype(F32) + dst
            sigma = 0.5 * jnp.tanh(0.5 * pre) + 0.5
            act = pre * sigma
            deriv[edge, rows, :] = (sigma + act * (1.0 - sigma)).astype(BF)
            total = act if total is None else total + act
        z = grid_ref[rows, :].astype(F32) + dot(total.astype(BF), w_msg_ref[...])
        centre = z - jnp.mean(z, axis=1, keepdims=True)
        scale = lax.rsqrt(jnp.mean(centre * centre, axis=1, keepdims=True) + LN_EPS)
        hat = centre * scale
        zhat[rows, :] = hat
        rstd[rows, :] = jnp.broadcast_to(scale, (chunk, LANES))
        pred[rows, :] = dot_t((hat * gain).astype(BF), w_out[...]).astype(BF)

    def pred_copy(part, other):
        return pltpu.make_async_remote_copy(
            src_ref=pred.at[pl.ds(part * chunk + other * share, share)],
            dst_ref=peers.at[me, pl.ds(part * share, share)],
            send_sem=pred_send.at[part, other],
            recv_sem=pred_recv.at[part, me],
            device_id={"member": other},
            device_id_type=MESH_ID,
        )

    def pred_arrival(part, other):
        return pltpu.make_async_remote_copy(
            src_ref=pred.at[pl.ds(part * chunk + other * share, share)],
            dst_ref=peers.at[other, pl.ds(part * share, share)],
            send_sem=pred_send.at[part, other],
            recv_sem=pred_recv.at[part, other],
            device_id={"member": other},
            device_id_type=MESH_ID,
        )

    def grad_copy(part, other):
        return pltpu.make_async_remote_copy(
            src_ref=d_peers.at[other, pl.ds(part * share, share)],
            dst_ref=d_pred.at[pl.ds(part * chunk + me * share, share)],
            send_sem=d_send.at[part, other],
            recv_sem=d_recv.at[part, me],
            device_id={"member": other},
            device_id_type=MESH_ID,
        )

    def grad_arrival(part, other):
        return pltpu.make_async_remote_copy(
            src_ref=d_peers.at[other, pl.ds(part * share, share)],
            dst_ref=d_pred.at[pl.ds(part * chunk + other * share, share)],
            send_sem=d_send.at[part, other],
            recv_sem=d_recv.at[part, other],
            device_id={"member": other},
            device_id_type=MESH_ID,
        )

    def others():
        return [lax.rem(me + step, n_member) for step in range(1, n_member)]

    def send_pred(part):
        for other in others():
            pred_copy(part, other).start()
        mine = pl.multiple_of(part * chunk + me * share, share)
        peers[me, part * share : (part + 1) * share, :] = pred[pl.ds(mine, share), :]

    def compare(part):
        for other in others():
            pred_arrival(part, other).wait_recv()
        rows = slice(part * share, (part + 1) * share)
        mine = pl.multiple_of(part * chunk + me * share, share)
        goal = table[pl.ds(mine, share), :]
        lane = lax.broadcasted_iota(jnp.int32, (share, LANES), 1)
        goal = jnp.where(lane < fields, goal, 0.0)
        values = [peers[member, rows, :].astype(F32) for member in range(n_member)]
        spread = [jnp.zeros((share, LANES), F32) for _ in range(n_member)]
        for left in range(n_member):
            for right in range(left + 1, n_member):
                step = slope(values[left] - values[right])
                spread[left] = spread[left] + step
                spread[right] = spread[right] - step
        for member in range(n_member):
            grad = weight_ref[...] * (slope(values[member] - goal) - coeff * spread[member])
            d_peers[member, rows, :] = grad.astype(BF)
        for other in others():
            grad_copy(part, other).start()
        d_pred[pl.ds(mine, share), :] = d_peers[me, rows, :]

    def backward(part):
        for other in others():
            grad_arrival(part, other).wait_recv()
        rows = pl.ds(part * chunk, chunk)
        hat = zhat[rows, :]
        scale = rstd[rows, 0:1]
        scaled = dot(d_pred[rows, :], w_out[...]) * gain
        d_z = scale * (
            scaled
            - jnp.mean(scaled, axis=1, keepdims=True)
            - hat * jnp.mean(scaled * hat, axis=1, keepdims=True)
        )
        d_act = dot_t(d_z.astype(BF), w_msg_ref[...])
        total = None
        for edge in range(edges):
            d_pre = (d_act * deriv[edge, rows, :].astype(F32)).astype(BF)
            deriv[edge, rows, :] = d_pre
            total = d_pre.astype(F32) if total is None else total + d_pre.astype(F32)
        d_grid_ref[rows, :] = (d_z + dot_t(total.astype(BF), w_dst_ref[...])).astype(BF)

    forward(0)
    send_pred(0)
    forward(1)
    send_pred(1)
    compare(0)
    forward(2)
    send_pred(2)
    compare(1)
    forward(3)
    send_pred(3)
    compare(2)
    backward(0)
    compare(3)
    backward(1)
    backward(2)
    backward(3)

    def scatter(first, height):
        total = None
        for edge in range(edges):
            part = dot(one_hot_rows(near_ref[edge : edge + 1, :], height, first), deriv[edge])
            total = part if total is None else total + part
        return total

    to_below = pltpu.make_async_remote_copy(
        src_ref=d_halo.at[0],
        dst_ref=back.at[pl.ds(rim, rim)],
        send_sem=back_send.at[0],
        recv_sem=back_recv.at[1],
        device_id={"band": jnp.maximum(band - 1, 0)},
        device_id_type=MESH_ID,
    )
    to_above = pltpu.make_async_remote_copy(
        src_ref=d_halo.at[1],
        dst_ref=back.at[pl.ds(0, rim)],
        send_sem=back_send.at[1],
        recv_sem=back_recv.at[0],
        device_id={"band": jnp.minimum(band + 1, n_band - 1)},
        device_id_type=MESH_ID,
    )
    d_halo[0] = scatter(owned, rim).astype(BF)

    @pl.when(has_below)
    def _():
        to_below.start()

    d_halo[1] = scatter(owned + rim, rim).astype(BF)

    @pl.when(has_above)
    def _():
        to_above.start()

    total = scatter(0, owned)

    @pl.when(has_above)
    def _():
        to_below.wait_recv()

    @pl.when(has_below)
    def _():
        to_above.wait_recv()

    for side in range(2):
        total = total + dot(
            one_hot_rows(send_ref[side : side + 1, :], owned, 0), back[side * rim : (side + 1) * rim, :]
        )
    d_mesh_ref[...] = dot_t(total.astype(BF), w_src_ref[...]).astype(BF)

    @pl.when(has_below)
    def _():
        down.wait_send()
        to_below.wait_send()

    @pl.when(has_above)
    def _():
        up.wait_send()
        to_above.wait_send()

    for part in range(CHUNKS):
        for other in others():
            pred_copy(part, other).wait_send()
            grad_copy(part, other).wait_send()


def per_device(
    n_band,
    n_member,
    grid_latent,
    mesh_latent,
    edge_attr,
    neighbours,
    send_rows,
    target,
    field_weight,
    w_src,
    w_dst,
    w_edge,
    w_msg,
    ln_gain,
    w_out,
):
    grid_rows = grid_latent[0]
    mesh_rows = mesh_latent[0]
    points, channels = grid_rows.shape
    owned = mesh_rows.shape[0]
    edges = neighbours.shape[1]
    rim = send_rows.shape[1]
    fields = target.shape[0]
    share = points // n_member
    weights = jnp.pad(field_weight, (0, LANES - fields)).reshape(1, LANES)
    vmem = pl.BlockSpec(memory_space=pltpu.VMEM)
    dma = pltpu.SemaphoreType.DMA
    d_grid, d_mesh = pl.pallas_call(
        functools.partial(kernel, n_band, n_member),
        out_shape=(
            jax.ShapeDtypeStruct((points, channels), BF),
            jax.ShapeDtypeStruct((owned, channels), BF),
        ),
        in_specs=[vmem] * 13,
        out_specs=(vmem, vmem),
        scratch_shapes=[
            pltpu.VMEM((LANES, points), F32),
            pltpu.VMEM((points, LANES), F32),
            pltpu.VMEM((LANES, channels), BF),
            pltpu.VMEM((owned, channels), BF),
            pltpu.VMEM((2, rim, channels), BF),
            pltpu.VMEM((2 * rim + LANES, channels), BF),
            pltpu.VMEM((edges, points, channels), BF),
            pltpu.VMEM((edges, points, channels), BF),
            pltpu.VMEM((points, channels), F32),
            pltpu.VMEM((points, LANES), F32),
            pltpu.VMEM((points, LANES), BF),
            pltpu.VMEM((n_member, share, LANES), BF),
            pltpu.VMEM((n_member, share, LANES), BF),
            pltpu.VMEM((points, LANES), BF),
            pltpu.VMEM((2, rim, channels), BF),
            pltpu.VMEM((2 * rim, channels), BF),
            dma((2,)),
            dma((2,)),
            dma((CHUNKS, n_member)),
            dma((CHUNKS, n_member)),
            dma((CHUNKS, n_member)),
            dma((CHUNKS, n_member)),
            dma((2,)),
            dma((2,)),
        ],
        compiler_params=pltpu.CompilerParams(
            collective_id=0, has_side_effects=True, vmem_limit_bytes=58 * 2**20
        ),
    )(
        grid_rows,
        mesh_rows,
        edge_attr,
        neighbours.T,
        send_rows,
        target,
        weights,
        w_src,
        w_dst,
        w_edge,
        w_msg,
        ln_gain.reshape(1, channels),
        w_out.T,
    )
    return d_grid[None], d_mesh[None]


def solution(mesh):
    placed = (
        P("member", "band", None),
        P("member", "band", None),
        P(None, None, "band"),
        P("band", None),
        P("band", None),
        P(None, "band"),
        P(),
        P(),
        P(),
        P(),
        P(),
        P(),
        P(),
    )
    return jax.shard_map(
        functools.partial(per_device, mesh.shape["band"], mesh.shape["member"]),
        mesh=mesh,
        in_specs=placed,
        out_specs=(P("member", "band", None), P("member", "band", None)),
        check_vma=False,
    )
```

time: 233 us -> 62.7 us (0.27)
  local copies, waits for them, and re-layouts: 76.5 us -> 4.48 us
  Pallas kernels: 0 us -> 57.5 us
  other arithmetic: 53.8 us -> 0 us
  waiting for transfers between devices: 50.4 us -> 0 us
  matrix products: 21.7 us -> 0 us
  starting transfers between devices: 14.3 us -> 0 us
  between operations: 14.4 us -> 0.66 us
    pallas_call x0 -> x1, Pallas kernels: none -> 57.5 us  [per_device(): pl.pallas_call(functools.partial(kernel, n_band, n_member), out_shape=(ja...]
    convert_element_type x4 -> x0, local copies, waits for them, and re-layouts: 36.8 us -> none  [the longest x2 18.4 us: per_device(): src_slots[neighbours].astype(jnp.float32) + dst[:, None, :] + edge_embed]
    all_gather x1 -> x0, waiting for transfers between devices: 36.4 us -> none  [per_device(): lax.all_gather(pred[None].astype(jnp.bfloat16), 'member', axis=0, tiled=T...]
    scatter-add x2 -> x0, other arithmetic: 35.7 us -> none  [the longest x1 27.4 us: per_device(): jax.ops.segment_sum(d_pre.reshape(points * edges, channels).astype(jnp.fl...]
    gather x2 -> x0, local copies, waits for them, and re-layouts: 22.7 us -> none  [the longest x1 17.4 us: per_device(): src_slots[neighbours].astype(jnp.float32) + dst[:, None, :] + edge_embed]
    dot_general x9 -> x0, matrix products: 21.7 us -> none  [the longest x3 8.49 us: times_transposed(): lax.dot_general(left, weight, (((1,), (1,)), ((), ())), preferred_element...]
    ppermute x4 -> x0, starting transfers between devices: 14.2 us -> none  [the longest x2 9.91 us: extended(): lax.ppermute(lax.slice_in_dim(block, 0, width, axis=dim), axis, backward)]
    ppermute x4 -> x0, waiting for transfers between devices: 14 us -> none  [the longest x2 12.9 us: extended(): lax.ppermute(lax.slice_in_dim(block, block.shape[dim] - width, None, axis...]
  transfers between devices with their start and end apart: 5 -> 0, of which waited for: 4 -> 0; matrix products, arithmetic and copies ran while one was open for 5% -> 0% of each run, Pallas kernels for 0% -> 0%
where the time goes in v1:
time: 62.7 us; the launch traced here: 62.6 us
  Pallas kernels  57.5 us (92%)
  local copies, waits for them, and re-layouts  4.48 us (7%)
  between operations  0.66 us (1%)
    pallas_call x1, Pallas kernels, per_device(): pl.pallas_call(functools.partial(kernel, n_band, n_member), out_shape=(ja...  57.5 us
    unnamed x6, local copies, waits for them, and re-layouts  3.97 us

profile of v1, /device:TPU:24, one launch (start us, length us, event | category | flops | bytes accessed | tf_op | source)
XLA Modules:
  0.0 62.6 jit_solution(17544053978474208248)
XLA Ops:
  0.6 0.0 copy-start.1
  0.6 0.6 %copy-done.1 = f32[100]{0:T(128)S(1)} copy-done((f32[100]{0:T(128)S(1)}, f32[100]{0:T(128)}, u32[]{:S(2)}) %copy-start.1) | copy-done | bytes 424
  1.3 0.5 pad_bitcast_fusion.weight_ref
  1.8 57.5 %shard_map.140 = (bf16[1024,512]{1,0:T(8,128)(2,1)}, bf16[1024,512]{1,0:T(8,128)(2,1)}) custom-call(bf16[1024,512]{1,0:T(8,128)(2,1)} %bitcast.11, bf16[1024,512]{1,0:T(8,128)(2,1)} %bitcast.12, bf16[4,4,1024]{2,1,0:T(4,128)(2,1)} %edge_ref.1, s32[4,1024]{1,0:T(4,128)} %bitcast.14, s32[2,512]{1,0:T(2,128)} %send_ref.1, f32[100,1024]{1,0:T(8,128)} %target_ref.1, ...), custom_call_target="tpu_custom_call" | custom-call | tf_op jit(solution)/shard_map/pallas_call | solution.py:450
  59.3 0.0 copy-start
  59.3 2.4 %copy.17 = bf16[1,1024,512]{2,1,0:T(8,128)(2,1)} copy(bf16[1,1024,512]{2,1,0:T(8,128)(2,1)} %bitcast.10) | data formatting | bytes 2097152
  61.6 0.0 copy-done
  61.6 1.0 %copy.18 = bf16[1,1024,512]{2,1,0:T(8,128)(2,1)} copy(bf16[1,1024,512]{2,1,0:T(8,128)(2,1)S(1)} %bitcast.9) | data formatting | bytes 2097152
Async XLA Ops:
  0.6 0.7 %copy-start.1 = (f32[100]{0:T(128)S(1)}, f32[100]{0:T(128)}, u32[]{:S(2)}) copy-start(f32[100]{0:T(128)} %param.19) | copy-start | bytes 1204
  59.3 2.4 %copy-start = (bf16[1024,512]{1,0:T(8,128)(2,1)S(1)}, bf16[1024,512]{1,0:T(8,128)(2,1)}, u32[]{:S(2)}) copy-start(bf16[1024,512]{1,0:T(8,128)(2,1)} %get-tuple-element.5) | copy-start | bytes 3145732

commit v2 on v0

v2 whole, which is shorter than its diff:
```python
import functools

import jax
import jax.numpy as jnp
from jax import lax
from jax.experimental import pallas as pl
from jax.experimental.pallas import tpu as pltpu
from jax.sharding import PartitionSpec as P

DELTA_SQ = 0.0625
ALPHA = 0.95
LN_EPS = 1e-05

BF = jnp.bfloat16
F32 = jnp.float32
LANES = 128
CHUNKS = 4
MESH_ID = pl.DeviceIdType.MESH

COL_KNOWN = 100
COL_EDGE = 104
COL_FAR = 120


def dot(left, right):
    return jnp.dot(left, right, preferred_element_type=F32)


def dot_t(left, right):
    return lax.dot_general(left, right, (((1,), (1,)), ((), ())), preferred_element_type=F32)


def slope(diff):
    return diff * lax.rsqrt(diff * diff + DELTA_SQ)


def one_hot_columns(column, width):
    rows = column.shape[0]
    return jnp.where(lax.broadcasted_iota(jnp.int32, (rows, width), 1) == column, 1.0, 0.0).astype(BF)


def one_hot_rows(row, height, first):
    width = row.shape[1]
    return jnp.where(
        lax.broadcasted_iota(jnp.int32, (height, width), 0) + first == row, 1.0, 0.0
    ).astype(BF)


def remote(src, dst, send_sem, recv_sem, **where):
    return pltpu.make_async_remote_copy(
        src_ref=src, dst_ref=dst, send_sem=send_sem, recv_sem=recv_sem, device_id=where, device_id_type=MESH_ID
    )


def kernel(n_band, n_member, *refs):
    hbm, (d_grid_hbm, total_hbm), refs = refs[:13], refs[13:15], refs[15:]
    held, refs = refs[:13], refs[13:]
    (
        grid_ref,
        mesh_ref,
        edge_ref,
        near_ref,
        send_ref,
        target_ref,
        weight_ref,
        w_src_ref,
        w_dst_ref,
        w_edge_ref,
        w_msg_ref,
        gain_ref,
        w_out_ref,
    ) = held
    (
        lists,
        wide,
        table,
        w_out,
        weights,
        columns,
        known,
        out_halo,
        away,
        base,
        read_even,
        read_odd,
        deriv,
        deriv_sum,
        zhat,
        rstd,
        pred,
        peers,
        d_peers,
        d_pred,
        d_sum,
        d_grid,
        slots,
        rims,
        d_halo,
        back,
        sums,
        load_sem,
        store_sem,
        halo_send,
        halo_recv,
        pred_send,
        pred_recv,
        d_send,
        d_recv,
        back_send,
        back_recv,
    ) = refs
    points, channels = grid_ref.shape
    owned = mesh_ref.shape[0]
    features = edge_ref.shape[0]
    edges = near_ref.shape[0]
    rim = send_ref.shape[1]
    fields = target_ref.shape[0]
    chunk = points // CHUNKS
    share = chunk // n_member
    band = lax.axis_index("band")
    me = lax.axis_index("member")
    has_below = band > 0
    has_above = band < n_band - 1
    far = lax.rem(band, 2)
    near = 1 - far
    has_far = ((far == 0) & has_below) | ((far == 1) & has_above)
    near_band = band + 2 * near - 1
    far_band = jnp.clip(band + 2 * far - 1, 0, n_band - 1)
    coeff = ALPHA / (n_member - 1) + (1.0 - ALPHA) / n_member

    def others():
        return [lax.rem(me + step, n_member) for step in range(1, n_member)]

    barrier = pltpu.get_barrier_semaphore()

    @pl.when(has_below)
    def _():
        pl.semaphore_signal(barrier, inc=1, device_id={"band": band - 1}, device_id_type=MESH_ID)

    @pl.when(has_above)
    def _():
        pl.semaphore_signal(barrier, inc=1, device_id={"band": band + 1}, device_id_type=MESH_ID)

    for other in others():
        pl.semaphore_signal(barrier, inc=1, device_id={"member": other}, device_id_type=MESH_ID)

    loads = [pltpu.make_async_copy(hbm[i], held[i], load_sem.at[i]) for i in range(13)]
    for i in (4, 1, 7, 3, 0, 8, 2, 5, 9, 10, 11, 12, 6):
        loads[i].start()

    loads[4].wait()
    lists[...] = jnp.zeros_like(lists)
    lists[0:1, 0:rim] = send_ref[0:1, :].astype(F32)
    lists[0:1, rim : 2 * rim] = send_ref[1:2, :].astype(F32)
    columns[...] = lists[...].T
    loads[1].wait()
    loads[7].wait()
    known[0:owned, :] = (0.5 * dot(mesh_ref[...], w_src_ref[...])).astype(BF)

    def select(side):
        rows = pl.ds(pl.multiple_of(side * rim, rim), rim)
        hot = one_hot_columns(columns[rows, 0:1].astype(jnp.int32), owned)
        return dot(hot, known[0:owned, :]).astype(BF)

    to_near = remote(
        out_halo.at[0], known.at[pl.ds(owned, rim)], halo_send.at[0], halo_recv.at[0], band=near_band
    )
    to_far = remote(out_halo.at[1], away.at[pl.ds(0, rim)], halo_send.at[1], halo_recv.at[1], band=far_band)
    out_halo[1] = select(far)
    pl.semaphore_wait(
        barrier, n_member - 1 + jnp.where(has_below, 1, 0) + jnp.where(has_above, 1, 0)
    )

    @pl.when(has_far)
    def _():
        to_far.start()

    out_halo[0] = select(near)
    to_near.start()

    @pl.when(jnp.logical_not(has_far))
    def _():
        away[0:rim, :] = jnp.zeros((rim, channels), BF)
        back[rim : 2 * rim, :] = jnp.zeros((rim, channels), BF)

    for i in (3, 2, 5, 9, 12, 6, 11):
        loads[i].wait()
    names = near_ref[...]
    in_near = (names >= owned + near * rim) & (names < owned + (near + 1) * rim)
    known_names = jnp.where(in_near, names - near * rim, jnp.where(names < owned, names, -1))
    wide[...] = jnp.zeros_like(wide)
    wide[0:fields, :] = target_ref[...]
    wide[COL_KNOWN : COL_KNOWN + edges, :] = known_names.astype(F32)
    wide[COL_FAR : COL_FAR + edges, :] = (names - owned - far * rim).astype(F32)
    for feature in range(features):
        wide[COL_EDGE + feature * edges : COL_EDGE + (feature + 1) * edges, :] = edge_ref[feature].astype(F32)
    table[...] = wide[...].T
    w_out[...] = jnp.zeros_like(w_out)
    w_out[0:fields, :] = w_out_ref[...]
    weights[...] = jnp.zeros_like(weights)
    weights[0:1, 0:fields] = weight_ref[...]
    away[rim:, :] = jnp.zeros((LANES, channels), BF)
    for feature in range(features):
        half = (0.5 * w_edge_ref[feature : feature + 1, :].astype(F32)).astype(BF)
        for edge in range(edges):
            row = rim + COL_EDGE + feature * edges + edge
            away[row : row + 1, :] = half
    loads[0].wait()
    loads[8].wait()
    zhat[...] = 0.5 * dot(grid_ref[...], w_dst_ref[...])
    to_near.wait_recv()

    def gather_known(part, _):
        rows = pl.ds(pl.multiple_of(part * chunk, chunk), chunk)
        hot = jnp.concatenate(
            [
                one_hot_columns(
                    table[rows, COL_KNOWN + edge : COL_KNOWN + edge + 1].astype(jnp.int32), owned + rim
                )
                for edge in range(edges)
            ],
            axis=0,
        )
        found = dot(hot, known[...])
        dst = zhat[rows, :]
        for edge in range(edges):
            base[edge, rows, :] = found[edge * chunk : (edge + 1) * chunk, :] + dst
        return 0

    lax.fori_loop(0, CHUNKS, gather_known, 0)
    loads[10].wait()

    @pl.when(has_far)
    def _():
        to_far.wait_recv()

    gain = gain_ref[...]
    reads = (read_even, read_odd)

    def read(part):
        rows = pl.ds(part * chunk, chunk)
        lane = lax.broadcasted_iota(jnp.int32, (chunk, LANES), 1)
        values = table[rows, :]
        hots = []
        for edge in range(edges):
            column = table[rows, COL_FAR + edge : COL_FAR + edge + 1].astype(jnp.int32)
            chosen = (lane >= COL_EDGE) & (lane < COL_FAR) & (lax.rem(lane, edges) == edge)
            hots.append(
                jnp.concatenate(
                    [
                        one_hot_columns(column, rim),
                        jnp.where(chosen, values, 0.0).astype(BF),
                    ],
                    axis=1,
                )
            )
        reads[part % 2][...] = dot(jnp.concatenate(hots, axis=0), away[...])

    def forward(part):
        rows = pl.ds(part * chunk, chunk)
        total = None
        derivs = None
        for edge in range(edges):
            half = reads[part % 2][edge * chunk : (edge + 1) * chunk, :] + base[edge, rows, :]
            rise = jnp.tanh(half) + 1.0
            act = half * rise
            twice = rise + act * (2.0 - rise)
            deriv[edge, rows, :] = twice.astype(BF)
            total = act if total is None else total + act
            derivs = twice if derivs is None else derivs + twice
        deriv_sum[rows, :] = derivs
        z = grid_ref[rows, :].astype(F32) + dot(total.astype(BF), w_msg_ref[...])
        centre = z - jnp.mean(z, axis=1, keepdims=True)
        scale = lax.rsqrt(jnp.mean(centre * centre, axis=1, keepdims=True) + LN_EPS)
        hat = centre * scale
        zhat[rows, :] = hat
        rstd[rows, :] = jnp.broadcast_to(scale, (chunk, LANES))
        pred[rows, :] = dot_t((hat * gain).astype(BF), w_out[...]).astype(BF)

    def pred_copy(part, other):
        return remote(
            pred.at[pl.ds(part * chunk + other * share, share)],
            peers.at[me, pl.ds(part * share, share)],
            pred_send,
            pred_recv.at[part],
            member=other,
        )

    def grad_copy(part, other):
        return remote(
            d_peers.at[other, pl.ds(part * share, share)],
            d_pred.at[pl.ds(part * chunk + me * share, share)],
            d_send,
            d_recv.at[part],
            member=other,
        )

    def all_of(count, send_sem, recv_sem):
        size = pl.ds(0, count * share)
        return remote(pred.at[size], d_pred.at[size], send_sem, recv_sem, member=lax.rem(me + 1, n_member))

    def send_pred(part):
        for other in others():
            pred_copy(part, other).start()
        mine = pl.multiple_of(part * chunk + me * share, share)
        peers[me, part * share : (part + 1) * share, :] = pred[pl.ds(mine, share), :]

    def compare(part):
        all_of(n_member - 1, pred_send, pred_recv.at[part]).wait_recv()
        rows = slice(part * share, (part + 1) * share)
        mine = pl.multiple_of(part * chunk + me * share, share)
        goal = table[pl.ds(mine, share), :]
        lane = lax.broadcasted_iota(jnp.int32, (share, LANES), 1)
        goal = jnp.where(lane < fields, goal, 0.0)
        values = [peers[member, rows, :].astype(F32) for member in range(n_member)]
        spread = [jnp.zeros((share, LANES), F32) for _ in range(n_member)]
        for left in range(n_member):
            for right in range(left + 1, n_member):
                step = slope(values[left] - values[right])
                spread[left] = spread[left] + step
                spread[right] = spread[right] - step
        for member in range(n_member):
            grad = weights[...] * (slope(values[member] - goal) - coeff * spread[member])
            d_peers[member, rows, :] = grad.astype(BF)
        for other in others():
            grad_copy(part, other).start()
        d_pred[pl.ds(mine, share), :] = d_peers[me, rows, :]

    def backward(part):
        all_of(n_member - 1, d_send, d_recv.at[part]).wait_recv()
        rows = pl.ds(part * chunk, chunk)
        hat = zhat[rows, :]
        scale = rstd[rows, 0:1]
        scaled = dot(d_pred[rows, :], w_out[...]) * gain
        d_z = scale * (
            scaled
            - jnp.mean(scaled, axis=1, keepdims=True)
            - hat * jnp.mean(scaled * hat, axis=1, keepdims=True)
        )
        zhat[rows, :] = d_z
        d_act = 0.5 * dot_t(d_z.astype(BF), w_msg_ref[...])
        d_sum[rows, :] = (d_act * deriv_sum[rows, :]).astype(BF)
        d_act = d_act.astype(BF)
        for edge in range(edges):
            deriv[edge, rows, :] = d_act * deriv[edge, rows, :]

    def scatter(part, parts, first, height):
        size = points // parts
        rows = pl.ds(part * size, size)
        names = jnp.concatenate([near_ref[edge : edge + 1, rows] for edge in range(edges)], axis=1)
        grads = jnp.concatenate([deriv[edge, rows, :] for edge in range(edges)], axis=0)
        return dot(one_hot_rows(names, height, first), grads)

    def scatter_far(part):
        found = scatter(part, CHUNKS, owned + far * rim, rim)
        if part == 0:
            rims[...] = found
        elif part < CHUNKS - 1:
            rims[...] += found
        else:
            d_halo[1] = (rims[...] + found).astype(BF)

    read(0)
    read(1)
    forward(0)
    send_pred(0)
    read(2)
    forward(1)
    send_pred(1)
    compare(0)
    read(3)
    forward(2)
    send_pred(2)
    compare(1)
    forward(3)
    send_pred(3)
    compare(2)
    backward(0)
    scatter_far(0)
    backward(1)
    scatter_far(1)
    compare(3)
    backward(2)
    scatter_far(2)
    backward(3)
    scatter_far(3)

    back_near = remote(
        d_halo.at[0], back.at[pl.ds(0, rim)], back_send.at[0], back_recv.at[0], band=near_band
    )
    back_far = remote(
        d_halo.at[1], back.at[pl.ds(rim, rim)], back_send.at[1], back_recv.at[1], band=far_band
    )

    @pl.when(has_far)
    def _():
        back_far.start()

    d_halo[0] = scatter(0, 1, owned + near * rim, rim).astype(BF)
    back_near.start()
    d_grid[...] = (zhat[...] + dot_t(d_sum[...], w_dst_ref[...])).astype(BF)
    grid_out = pltpu.make_async_copy(d_grid, d_grid_hbm, store_sem.at[0])
    grid_out.start()
    slots[...] = scatter(0, 1, 0, owned)

    def returned(side, place):
        return dot(
            one_hot_rows(send_ref[pl.ds(side, 1), :], owned, 0), back[place * rim : (place + 1) * rim, :]
        )

    back_near.wait_recv()
    slots[...] += returned(near, 0)

    @pl.when(has_far)
    def _():
        back_far.wait_recv()

    sums[...] = (slots[...] + returned(far, 1)).astype(BF)
    total_out = pltpu.make_async_copy(sums, total_hbm, store_sem.at[1])
    total_out.start()

    to_near.wait_send()
    back_near.wait_send()

    @pl.when(has_far)
    def _():
        to_far.wait_send()
        back_far.wait_send()

    all_of(CHUNKS * (n_member - 1), pred_send, pred_recv.at[0]).wait_send()
    all_of(CHUNKS * (n_member - 1), d_send, d_recv.at[0]).wait_send()
    grid_out.wait()
    total_out.wait()


def finish(grid_in, sums_hbm, w_src_hbm, grid_out, mesh_out, sums, w_src, rows_out, load_sem, store_sem):
    through = pltpu.make_async_copy(grid_in, grid_out, store_sem.at[0])
    weight = pltpu.make_async_copy(w_src_hbm, w_src, load_sem.at[0])
    values = pltpu.make_async_copy(sums_hbm, sums, load_sem.at[1])
    weight.start()
    values.start()
    through.start()
    weight.wait()
    values.wait()
    height = sums.shape[0] // 2
    stores = []
    for part in range(2):
        rows = pl.ds(part * height, height)
        rows_out[rows, :] = dot_t(sums[rows, :], w_src[...]).astype(BF)
        stores.append(
            pltpu.make_async_copy(rows_out.at[rows], mesh_out.at[rows], store_sem.at[part + 1])
        )
        stores[-1].start()
    through.wait()
    for store in stores:
        store.wait()


def per_device(
    n_band,
    n_member,
    grid_latent,
    mesh_latent,
    edge_attr,
    neighbours,
    send_rows,
    target,
    field_weight,
    w_src,
    w_dst,
    w_edge,
    w_msg,
    ln_gain,
    w_out,
):
    grid_rows = grid_latent[0]
    mesh_rows = mesh_latent[0]
    points, channels = grid_rows.shape
    owned = mesh_rows.shape[0]
    edges = neighbours.shape[1]
    rim = send_rows.shape[1]
    fields = target.shape[0]
    share = points // n_member
    chunk = points // CHUNKS
    operands = (
        grid_rows,
        mesh_rows,
        edge_attr,
        neighbours.T,
        send_rows,
        target,
        field_weight.reshape(1, fields),
        w_src,
        w_dst,
        w_edge,
        w_msg,
        ln_gain.reshape(1, channels),
        w_out.T,
    )
    anywhere = pl.BlockSpec(memory_space=pl.ANY)
    dma = pltpu.SemaphoreType.DMA
    latents = pltpu.VMEM((points, channels), BF)
    wide_latents = pltpu.VMEM((points, channels), F32)
    d_grid, sums = pl.pallas_call(
        functools.partial(kernel, n_band, n_member),
        out_shape=(
            jax.ShapeDtypeStruct((points, channels), BF),
            jax.ShapeDtypeStruct((owned, channels), BF),
        ),
        in_specs=[anywhere] * len(operands),
        out_specs=(anywhere, anywhere),
        scratch_shapes=[pltpu.VMEM(operand.shape, operand.dtype) for operand in operands]
        + [
            pltpu.VMEM((8, 2 * rim), F32),
            pltpu.VMEM((LANES, points), F32),
            pltpu.VMEM((points, LANES), F32),
            pltpu.VMEM((LANES, channels), BF),
            pltpu.VMEM((1, LANES), F32),
            pltpu.VMEM((2 * rim, 8), F32),
            pltpu.VMEM((owned + rim, channels), BF),
            pltpu.VMEM((2, rim, channels), BF),
            pltpu.VMEM((rim + LANES, channels), BF),
            pltpu.VMEM((edges, points, channels), F32),
            pltpu.VMEM((edges * chunk, channels), F32),
            pltpu.VMEM((edges * chunk, channels), F32),
            pltpu.VMEM((edges, points, channels), BF),
            wide_latents,
            wide_latents,
            pltpu.VMEM((points, LANES), F32),
            pltpu.VMEM((points, LANES), BF),
            pltpu.VMEM((n_member, share, LANES), BF),
            pltpu.VMEM((n_member, share, LANES), BF),
            pltpu.VMEM((points, LANES), BF),
            latents,
            latents,
            wide_latents,
            pltpu.VMEM((rim, channels), F32),
            pltpu.VMEM((2, rim, channels), BF),
            pltpu.VMEM((2 * rim, channels), BF),
            latents,
            dma((len(operands),)),
            dma((2,)),
            dma((2,)),
            dma((2,)),
            dma,
            dma((CHUNKS,)),
            dma,
            dma((CHUNKS,)),
            dma((2,)),
            dma((2,)),
        ],
        compiler_params=pltpu.CompilerParams(
            collective_id=0, has_side_effects=True, vmem_limit_bytes=58 * 2**20
        ),
    )(*operands)
    d_grid, d_mesh = pl.pallas_call(
        finish,
        out_shape=(
            jax.ShapeDtypeStruct((points, channels), BF),
            jax.ShapeDtypeStruct((owned, channels), BF),
        ),
        in_specs=[anywhere] * 3,
        out_specs=(anywhere, anywhere),
        scratch_shapes=[latents, pltpu.VMEM(w_src.shape, BF), latents, dma((2,)), dma((3,))],
        compiler_params=pltpu.CompilerParams(vmem_limit_bytes=16 * 2**20),
    )(d_grid, sums, w_src)
    return d_grid[None], d_mesh[None]


def solution(mesh):
    placed = (
        P("member", "band", None),
        P("member", "band", None),
        P(None, None, "band"),
        P("band", None),
        P("band", None),
        P(None, "band"),
        P(),
        P(),
        P(),
        P(),
        P(),
        P(),
        P(),
    )
    return jax.shard_map(
        functools.partial(per_device, mesh.shape["band"], mesh.shape["member"]),
        mesh=mesh,
        in_specs=placed,
        out_specs=(P("member", "band", None), P("member", "band", None)),
        check_vma=False,
    )
```

time: 233 us -> 53.9 us (0.23)
  local copies, waits for them, and re-layouts: 76.5 us -> 2.45 us
  other arithmetic: 53.8 us -> 0 us
  waiting for transfers between devices: 50.4 us -> 0 us
  Pallas kernels: 0 us -> 50.1 us
  matrix products: 21.7 us -> 0 us
  starting transfers between devices: 14.3 us -> 0 us
  between operations: 14.4 us -> 0.85 us
    pallas_call x0 -> x2, Pallas kernels: none -> 50.1 us  [the longest x1 48.4 us: per_device(): pl.pallas_call(functools.partial(kernel, n_band, n_member), out_shape=(ja...]
    convert_element_type x4 -> x0, local copies, waits for them, and re-layouts: 36.8 us -> none  [the longest x2 18.4 us: per_device(): src_slots[neighbours].astype(jnp.float32) + dst[:, None, :] + edge_embed]
    all_gather x1 -> x0, waiting for transfers between devices: 36.4 us -> none  [per_device(): lax.all_gather(pred[None].astype(jnp.bfloat16), 'member', axis=0, tiled=T...]
    scatter-add x2 -> x0, other arithmetic: 35.7 us -> none  [the longest x1 27.4 us: per_device(): jax.ops.segment_sum(d_pre.reshape(points * edges, channels).astype(jnp.fl...]
    gather x2 -> x0, local copies, waits for them, and re-layouts: 22.7 us -> none  [the longest x1 17.4 us: per_device(): src_slots[neighbours].astype(jnp.float32) + dst[:, None, :] + edge_embed]
    dot_general x9 -> x0, matrix products: 21.7 us -> none  [the longest x3 8.49 us: times_transposed(): lax.dot_general(left, weight, (((1,), (1,)), ((), ())), preferred_element...]
    ppermute x4 -> x0, starting transfers between devices: 14.2 us -> none  [the longest x2 9.91 us: extended(): lax.ppermute(lax.slice_in_dim(block, 0, width, axis=dim), axis, backward)]
    ppermute x4 -> x0, waiting for transfers between devices: 14 us -> none  [the longest x2 12.9 us: extended(): lax.ppermute(lax.slice_in_dim(block, block.shape[dim] - width, None, axis...]
  transfers between devices with their start and end apart: 5 -> 0, of which waited for: 4 -> 0; matrix products, arithmetic and copies ran while one was open for 5% -> 0% of each run, Pallas kernels for 0% -> 0%
where the time goes in v2:
time: 53.9 us; the launch traced here: 53.4 us
  Pallas kernels  50.1 us (93%)
  local copies, waits for them, and re-layouts  2.45 us (5%)
  between operations  0.85 us (2%)
    pallas_call x1, Pallas kernels, per_device(): pl.pallas_call(functools.partial(kernel, n_band, n_member), out_shape=(ja...  48.4 us
    unnamed x6, local copies, waits for them, and re-layouts  2.45 us
    pallas_call x1, Pallas kernels, per_device(): pl.pallas_call(finish, out_shape=(jax.ShapeDtypeStruct((points, channels)...  1.69 us

profile of v2, /device:TPU:24, one launch (start us, length us, event | category | flops | bytes accessed | tf_op | source)
XLA Modules:
  0.0 53.4 jit_solution(16612340507830892756)
XLA Ops:
  0.6 0.0 copy-start
  0.6 48.4 %shard_map.140 = (bf16[1024,512]{1,0:T(8,128)(2,1)}, bf16[1024,512]{1,0:T(8,128)(2,1)}) custom-call(bf16[1024,512]{1,0:T(8,128)(2,1)} %bitcast.8, bf16[1024,512]{1,0:T(8,128)(2,1)} %bitcast.9, bf16[4,4,1024]{2,1,0:T(4,128)(2,1)} %refs_2_.1, s32[4,1024]{1,0:T(4,128)} %bitcast.11, s32[2,512]{1,0:T(2,128)} %refs_4_.1, f32[100,1024]{1,0:T(8,128)} %refs_5_.1, ...), custom_call_target="tpu_custom_call" | custom-call | tf_op jit(solution)/shard_map/pallas_call | solution.py:504
  49.1 0.0 copy-done
  49.1 0.0 copy-start.1
  49.1 1.2 %copy-done.1 = bf16[1024,512]{1,0:T(8,128)(2,1)S(1)} copy-done((bf16[1024,512]{1,0:T(8,128)(2,1)S(1)}, bf16[1024,512]{1,0:T(8,128)(2,1)}, u32[]{:S(2)}) %copy-start.1) | copy-done | bytes 1048600
  50.3 0.0 copy-start.2
  50.3 1.2 %copy-done.2 = bf16[1024,512]{1,0:T(8,128)(2,1)S(1)} copy-done((bf16[1024,512]{1,0:T(8,128)(2,1)S(1)}, bf16[1024,512]{1,0:T(8,128)(2,1)}, u32[]{:S(2)}) %copy-start.2) | copy-done | bytes 1048600
  51.5 1.7 %shard_map.141 = (bf16[1024,512]{1,0:T(8,128)(2,1)}, bf16[1024,512]{1,0:T(8,128)(2,1)}) custom-call(bf16[1024,512]{1,0:T(8,128)(2,1)S(1)} %copy-done.1, bf16[1024,512]{1,0:T(8,128)(2,1)S(1)} %copy-done.2, bf16[512,512]{1,0:T(8,128)(2,1)S(1)} %copy-done), custom_call_target="tpu_custom_call" | custom-call | tf_op jit(solution)/shard_map/pallas_call | solution.py:556
Async XLA Ops:
  0.6 48.4 %copy-start = (bf16[512,512]{1,0:T(8,128)(2,1)S(1)}, bf16[512,512]{1,0:T(8,128)(2,1)}, u32[]{:S(2)}) copy-start(bf16[512,512]{1,0:T(8,128)(2,1)} %w_src_hbm.1) | copy-start | bytes 1572868
  49.1 1.2 %copy-start.1 = (bf16[1024,512]{1,0:T(8,128)(2,1)S(1)}, bf16[1024,512]{1,0:T(8,128)(2,1)}, u32[]{:S(2)}) copy-start(bf16[1024,512]{1,0:T(8,128)(2,1)} %get-tuple-element.6.grid_in) | copy-start | bytes 3145732
  50.3 1.2 %copy-start.2 = (bf16[1024,512]{1,0:T(8,128)(2,1)S(1)}, bf16[1024,512]{1,0:T(8,128)(2,1)}, u32[]{:S(2)}) copy-start(bf16[1024,512]{1,0:T(8,128)(2,1)} %get-tuple-element.7.sums_hbm) | copy-start | bytes 3145732

commit v3 on v2

--- a/solution.py
+++ b/solution.py
@@ -14,7 +14,8 @@
 BF = jnp.bfloat16
 F32 = jnp.float32
 LANES = 128
-CHUNKS = 4
+PARTS = (3, 3, 2)
+UNIT = 128
 MESH_ID = pl.DeviceIdType.MESH
 
 COL_KNOWN = 100
@@ -53,7 +54,7 @@
 
 
 def kernel(n_band, n_member, *refs):
-    hbm, (d_grid_hbm, total_hbm), refs = refs[:13], refs[13:15], refs[15:]
+    hbm, (d_grid, sums), refs = refs[:13], refs[13:15], refs[15:]
     held, refs = refs[:13], refs[13:]
     (
         grid_ref,
@@ -92,14 +93,11 @@
         d_peers,
         d_pred,
         d_sum,
-        d_grid,
         slots,
         rims,
         d_halo,
         back,
-        sums,
         load_sem,
-        store_sem,
         halo_send,
         halo_recv,
         pred_send,
@@ -115,8 +113,10 @@
     edges = near_ref.shape[0]
     rim = send_ref.shape[1]
     fields = target_ref.shape[0]
-    chunk = points // CHUNKS
-    share = chunk // n_member
+    firsts = [sum(PARTS[:part]) * UNIT for part in range(len(PARTS))]
+    sizes = [part * UNIT for part in PARTS]
+    shares = [size // n_member for size in sizes]
+    owns = [first // n_member for first in firsts]
     band = lax.axis_index("band")
     me = lax.axis_index("member")
     has_below = band > 0
@@ -210,8 +210,8 @@
     zhat[...] = 0.5 * dot(grid_ref[...], w_dst_ref[...])
     to_near.wait_recv()
 
-    def gather_known(part, _):
-        rows = pl.ds(pl.multiple_of(part * chunk, chunk), chunk)
+    def gather_known(part):
+        rows = pl.ds(firsts[part], sizes[part])
         hot = jnp.concatenate(
             [
                 one_hot_columns(
@@ -224,10 +224,10 @@
         found = dot(hot, known[...])
         dst = zhat[rows, :]
         for edge in range(edges):
-            base[edge, rows, :] = found[edge * chunk : (edge + 1) * chunk, :] + dst
-        return 0
-
-    lax.fori_loop(0, CHUNKS, gather_known, 0)
+            base[edge, rows, :] = found[edge * sizes[part] : (edge + 1) * sizes[part], :] + dst
+
+    gather_known(0)
+    gather_known(1)
     loads[10].wait()
 
     @pl.when(has_far)
@@ -238,8 +238,8 @@
     reads = (read_even, read_odd)
 
     def read(part):
-        rows = pl.ds(part * chunk, chunk)
-        lane = lax.broadcasted_iota(jnp.int32, (chunk, LANES), 1)
+        rows = pl.ds(firsts[part], sizes[part])
+        lane = lax.broadcasted_iota(jnp.int32, (sizes[part], LANES), 1)
         values = table[rows, :]
         hots = []
         for edge in range(edges):
@@ -254,14 +254,14 @@
                     axis=1,
                 )
             )
-        reads[part % 2][...] = dot(jnp.concatenate(hots, axis=0), away[...])
+        reads[part % 2][0 : edges * sizes[part], :] = dot(jnp.concatenate(hots, axis=0), away[...])
 
     def forward(part):
-        rows = pl.ds(part * chunk, chunk)
+        rows = pl.ds(firsts[part], sizes[part])
         total = None
         derivs = None
         for edge in range(edges):
-            half = reads[part % 2][edge * chunk : (edge + 1) * chunk, :] + base[edge, rows, :]
+            half = reads[part % 2][edge * sizes[part] : (edge + 1) * sizes[part], :] + base[edge, rows, :]
             rise = jnp.tanh(half) + 1.0
             act = half * rise
             twice = rise + act * (2.0 - rise)
@@ -274,13 +274,13 @@
         scale = lax.rsqrt(jnp.mean(centre * centre, axis=1, keepdims=True) + LN_EPS)
         hat = centre * scale
         zhat[rows, :] = hat
-        rstd[rows, :] = jnp.broadcast_to(scale, (chunk, LANES))
+        rstd[rows, :] = jnp.broadcast_to(scale, (sizes[part], LANES))
         pred[rows, :] = dot_t((hat * gain).astype(BF), w_out[...]).astype(BF)
 
     def pred_copy(part, other):
         return remote(
-            pred.at[pl.ds(part * chunk + other * share, share)],
-            peers.at[me, pl.ds(part * share, share)],
+            pred.at[pl.ds(firsts[part] + other * shares[part], shares[part])],
+            peers.at[me, pl.ds(owns[part], shares[part])],
             pred_send,
             pred_recv.at[part],
             member=other,
@@ -288,28 +288,29 @@
 
     def grad_copy(part, other):
         return remote(
-            d_peers.at[other, pl.ds(part * share, share)],
-            d_pred.at[pl.ds(part * chunk + me * share, share)],
+            d_peers.at[other, pl.ds(owns[part], shares[part])],
+            d_pred.at[pl.ds(firsts[part] + me * shares[part], shares[part])],
             d_send,
             d_recv.at[part],
             member=other,
         )
 
     def all_of(count, send_sem, recv_sem):
-        size = pl.ds(0, count * share)
+        size = pl.ds(0, count)
         return remote(pred.at[size], d_pred.at[size], send_sem, recv_sem, member=lax.rem(me + 1, n_member))
 
     def send_pred(part):
         for other in others():
             pred_copy(part, other).start()
-        mine = pl.multiple_of(part * chunk + me * share, share)
-        peers[me, part * share : (part + 1) * share, :] = pred[pl.ds(mine, share), :]
+        mine = pl.ds(pl.multiple_of(firsts[part] + me * shares[part], 16), shares[part])
+        peers[me, pl.ds(owns[part], shares[part]), :] = pred[mine, :]
 
     def compare(part):
-        all_of(n_member - 1, pred_send, pred_recv.at[part]).wait_recv()
-        rows = slice(part * share, (part + 1) * share)
-        mine = pl.multiple_of(part * chunk + me * share, share)
-        goal = table[pl.ds(mine, share), :]
+        all_of((n_member - 1) * shares[part], pred_send, pred_recv.at[part]).wait_recv()
+        share = shares[part]
+        rows = pl.ds(owns[part], share)
+        mine = pl.ds(pl.multiple_of(firsts[part] + me * share, 16), share)
+        goal = table[mine, :]
         lane = lax.broadcasted_iota(jnp.int32, (share, LANES), 1)
         goal = jnp.where(lane < fields, goal, 0.0)
         values = [peers[member, rows, :].astype(F32) for member in range(n_member)]
@@ -324,11 +325,11 @@
             d_peers[member, rows, :] = grad.astype(BF)
         for other in others():
             grad_copy(part, other).start()
-        d_pred[pl.ds(mine, share), :] = d_peers[me, rows, :]
+        d_pred[mine, :] = d_peers[me, rows, :]
 
     def backward(part):
-        all_of(n_member - 1, d_send, d_recv.at[part]).wait_recv()
-        rows = pl.ds(part * chunk, chunk)
+        all_of((n_member - 1) * shares[part], d_send, d_recv.at[part]).wait_recv()
+        rows = pl.ds(firsts[part], sizes[part])
         hat = zhat[rows, :]
         scale = rstd[rows, 0:1]
         scaled = dot(d_pred[rows, :], w_out[...]) * gain
@@ -344,46 +345,36 @@
         for edge in range(edges):
             deriv[edge, rows, :] = d_act * deriv[edge, rows, :]
 
-    def scatter(part, parts, first, height):
-        size = points // parts
-        rows = pl.ds(part * size, size)
+    def scatter(first_part, last_part, first, height):
+        rows = pl.ds(firsts[first_part], firsts[last_part] + sizes[last_part] - firsts[first_part])
         names = jnp.concatenate([near_ref[edge : edge + 1, rows] for edge in range(edges)], axis=1)
         grads = jnp.concatenate([deriv[edge, rows, :] for edge in range(edges)], axis=0)
         return dot(one_hot_rows(names, height, first), grads)
 
     def scatter_far(part):
-        found = scatter(part, CHUNKS, owned + far * rim, rim)
-        if part == 0:
-            rims[...] = found
-        elif part < CHUNKS - 1:
-            rims[...] += found
-        else:
-            d_halo[1] = (rims[...] + found).astype(BF)
+        return scatter(part, part, owned + far * rim, rim)
 
     read(0)
-    read(1)
     forward(0)
     send_pred(0)
-    read(2)
+    read(1)
     forward(1)
     send_pred(1)
     compare(0)
-    read(3)
+    gather_known(2)
+    read(2)
     forward(2)
     send_pred(2)
     compare(1)
-    forward(3)
-    send_pred(3)
+    backward(0)
+    rims[...] = scatter_far(0)
+    slots[...] = scatter(0, 0, 0, owned)
     compare(2)
-    backward(0)
-    scatter_far(0)
     backward(1)
-    scatter_far(1)
-    compare(3)
+    rims[...] += scatter_far(1)
+    slots[...] += scatter(1, 1, 0, owned)
     backward(2)
-    scatter_far(2)
-    backward(3)
-    scatter_far(3)
+    d_halo[1] = (rims[...] + scatter_far(2)).astype(BF)
 
     back_near = remote(
         d_halo.at[0], back.at[pl.ds(0, rim)], back_send.at[0], back_recv.at[0], band=near_band
@@ -396,12 +387,10 @@
     def _():
         back_far.start()
 
-    d_halo[0] = scatter(0, 1, owned + near * rim, rim).astype(BF)
+    d_halo[0] = scatter(0, 2, owned + near * rim, rim).astype(BF)
     back_near.start()
     d_grid[...] = (zhat[...] + dot_t(d_sum[...], w_dst_ref[...])).astype(BF)
-    grid_out = pltpu.make_async_copy(d_grid, d_grid_hbm, store_sem.at[0])
-    grid_out.start()
-    slots[...] = scatter(0, 1, 0, owned)
+    slots[...] += scatter(2, 2, 0, owned)
 
     def returned(side, place):
         return dot(
@@ -416,8 +405,6 @@
         back_far.wait_recv()
 
     sums[...] = (slots[...] + returned(far, 1)).astype(BF)
-    total_out = pltpu.make_async_copy(sums, total_hbm, store_sem.at[1])
-    total_out.start()
 
     to_near.wait_send()
     back_near.wait_send()
@@ -427,21 +414,13 @@
         to_far.wait_send()
         back_far.wait_send()
 
-    all_of(CHUNKS * (n_member - 1), pred_send, pred_recv.at[0]).wait_send()
-    all_of(CHUNKS * (n_member - 1), d_send, d_recv.at[0]).wait_send()
-    grid_out.wait()
-    total_out.wait()
-
-
-def finish(grid_in, sums_hbm, w_src_hbm, grid_out, mesh_out, sums, w_src, rows_out, load_sem, store_sem):
-    through = pltpu.make_async_copy(grid_in, grid_out, store_sem.at[0])
-    weight = pltpu.make_async_copy(w_src_hbm, w_src, load_sem.at[0])
-    values = pltpu.make_async_copy(sums_hbm, sums, load_sem.at[1])
-    weight.start()
-    values.start()
+    all_of((n_member - 1) * sum(shares), pred_send, pred_recv.at[0]).wait_send()
+    all_of((n_member - 1) * sum(shares), d_send, d_recv.at[0]).wait_send()
+
+
+def finish(d_grid, sums, w_src, grid_out, mesh_out, rows_out, store_sem):
+    through = pltpu.make_async_copy(d_grid, grid_out, store_sem.at[0])
     through.start()
-    weight.wait()
-    values.wait()
     height = sums.shape[0] // 2
     stores = []
     for part in range(2):
@@ -481,7 +460,7 @@
     rim = send_rows.shape[1]
     fields = target.shape[0]
     share = points // n_member
-    chunk = points // CHUNKS
+    largest = max(PARTS) * UNIT
     operands = (
         grid_rows,
         mesh_rows,
@@ -498,17 +477,15 @@
         w_out.T,
     )
     anywhere = pl.BlockSpec(memory_space=pl.ANY)
+    vmem = pl.BlockSpec(memory_space=pltpu.VMEM)
     dma = pltpu.SemaphoreType.DMA
     latents = pltpu.VMEM((points, channels), BF)
     wide_latents = pltpu.VMEM((points, channels), F32)
     d_grid, sums = pl.pallas_call(
         functools.partial(kernel, n_band, n_member),
-        out_shape=(
-            jax.ShapeDtypeStruct((points, channels), BF),
-            jax.ShapeDtypeStruct((owned, channels), BF),
-        ),
+        out_shape=(pltpu.VMEM((points, channels), BF), pltpu.VMEM((owned, channels), BF)),
         in_specs=[anywhere] * len(operands),
-        out_specs=(anywhere, anywhere),
+        out_specs=(vmem, vmem),
         scratch_shapes=[pltpu.VMEM(operand.shape, operand.dtype) for operand in operands]
         + [
             pltpu.VMEM((8, 2 * rim), F32),
@@ -521,8 +498,8 @@
             pltpu.VMEM((2, rim, channels), BF),
             pltpu.VMEM((rim + LANES, channels), BF),
             pltpu.VMEM((edges, points, channels), F32),
-            pltpu.VMEM((edges * chunk, channels), F32),
-            pltpu.VMEM((edges * chunk, channels), F32),
+            pltpu.VMEM((edges * largest, channels), F32),
+            pltpu.VMEM((edges * largest, channels), F32),
             pltpu.VMEM((edges, points, channels), BF),
             wide_latents,
             wide_latents,
@@ -532,25 +509,22 @@
             pltpu.VMEM((n_member, share, LANES), BF),
             pltpu.VMEM((points, LANES), BF),
             latents,
-            latents,
             wide_latents,
             pltpu.VMEM((rim, channels), F32),
             pltpu.VMEM((2, rim, channels), BF),
             pltpu.VMEM((2 * rim, channels), BF),
-            latents,
             dma((len(operands),)),
             dma((2,)),
             dma((2,)),
-            dma((2,)),
             dma,
-            dma((CHUNKS,)),
+            dma((len(PARTS),)),
             dma,
-            dma((CHUNKS,)),
+            dma((len(PARTS),)),
             dma((2,)),
             dma((2,)),
         ],
         compiler_params=pltpu.CompilerParams(
-            collective_id=0, has_side_effects=True, vmem_limit_bytes=58 * 2**20
+            collective_id=0, has_side_effects=True, vmem_limit_bytes=52 * 2**20
         ),
     )(*operands)
     d_grid, d_mesh = pl.pallas_call(
@@ -559,9 +533,9 @@
             jax.ShapeDtypeStruct((points, channels), BF),
             jax.ShapeDtypeStruct((owned, channels), BF),
         ),
-        in_specs=[anywhere] * 3,
+        in_specs=[vmem] * 3,
         out_specs=(anywhere, anywhere),
-        scratch_shapes=[latents, pltpu.VMEM(w_src.shape, BF), latents, dma((2,)), dma((3,))],
+        scratch_shapes=[latents, dma((3,))],
         compiler_params=pltpu.CompilerParams(vmem_limit_bytes=16 * 2**20),
     )(d_grid, sums, w_src)
     return d_grid[None], d_mesh[None]

time: 53.9 us -> 48.9 us (0.907)
  local copies, waits for them, and re-layouts: 2.45 us -> 0.01 us
  Pallas kernels: 50.1 us -> 48 us
    unnamed x6 -> x2, local copies, waits for them, and re-layouts: 2.45 us -> 0.01 us
    pallas_call x1, Pallas kernels: 48.4 us -> 46.3 us  [per_device(): pl.pallas_call(functools.partial(kernel, n_band, n_member), out_shape=(pl...]
where the time goes in v3:
time: 48.9 us; the launch traced here: 48.8 us
  Pallas kernels  48 us (98%)
  between operations  0.82 us (2%)
    pallas_call x1, Pallas kernels, per_device(): pl.pallas_call(functools.partial(kernel, n_band, n_member), out_shape=(pl...  46.3 us
    pallas_call x1, Pallas kernels, per_device(): pl.pallas_call(finish, out_shape=(jax.ShapeDtypeStruct((points, channels)...  1.75 us

profile of v3, /device:TPU:24, one launch (start us, length us, event | category | flops | bytes accessed | tf_op | source)
XLA Modules:
  0.0 48.8 jit_solution(16573384318318242782)
XLA Ops:
  0.6 0.0 copy-start
  0.6 46.3 %shard_map.140 = (bf16[1024,512]{1,0:T(8,128)(2,1)S(1)}, bf16[1024,512]{1,0:T(8,128)(2,1)S(1)}) custom-call(bf16[1024,512]{1,0:T(8,128)(2,1)} %bitcast.8, bf16[1024,512]{1,0:T(8,128)(2,1)} %bitcast.9, bf16[4,4,1024]{2,1,0:T(4,128)(2,1)} %refs_2_.1, s32[4,1024]{1,0:T(4,128)} %bitcast.11, s32[2,512]{1,0:T(2,128)} %refs_4_.1, f32[100,1024]{1,0:T(8,128)} %refs_5_.1, ...), custom_call_target="tpu_custom_call" | custom-call | tf_op jit(solution)/shard_map/pallas_call | solution.py:484
  46.9 0.0 copy-done
  46.9 1.7 %shard_map.141 = (bf16[1024,512]{1,0:T(8,128)(2,1)}, bf16[1024,512]{1,0:T(8,128)(2,1)}) custom-call(bf16[1024,512]{1,0:T(8,128)(2,1)S(1)} %get-tuple-element.6.d_grid, bf16[1024,512]{1,0:T(8,128)(2,1)S(1)} %get-tuple-element.7.sums, bf16[512,512]{1,0:T(8,128)(2,1)S(1)} %copy-done), custom_call_target="tpu_custom_call" | custom-call | tf_op jit(solution)/shard_map/pallas_call | solution.py:530
Async XLA Ops:
  0.6 46.3 %copy-start = (bf16[512,512]{1,0:T(8,128)(2,1)S(1)}, bf16[512,512]{1,0:T(8,128)(2,1)}, u32[]{:S(2)}) copy-start(bf16[512,512]{1,0:T(8,128)(2,1)} %w_src.1) | copy-start | bytes 1572868

commit v4 on v3

--- a/solution.py
+++ b/solution.py
@@ -129,7 +129,13 @@
     coeff = ALPHA / (n_member - 1) + (1.0 - ALPHA) / n_member
 
     def others():
-        return [lax.rem(me + step, n_member) for step in range(1, n_member)]
+        ring = n_member // 2
+        along, row = lax.rem(me, ring), me // ring
+        hops = sorted(
+            ((dy, dx) for dy in range(2) for dx in range(ring) if dy + dx > 0),
+            key=lambda hop: -(hop[0] + min(hop[1], ring - hop[1])),
+        )
+        return [lax.rem(row + dy, 2) * ring + lax.rem(along + dx, ring) for dy, dx in hops]
 
     barrier = pltpu.get_barrier_semaphore()
 
@@ -145,7 +151,7 @@
         pl.semaphore_signal(barrier, inc=1, device_id={"member": other}, device_id_type=MESH_ID)
 
     loads = [pltpu.make_async_copy(hbm[i], held[i], load_sem.at[i]) for i in range(13)]
-    for i in (4, 1, 7, 3, 0, 8, 2, 5, 9, 10, 11, 12, 6):
+    for i in (4, 7, 1):
         loads[i].start()
 
     loads[4].wait()
@@ -153,29 +159,44 @@
     lists[0:1, 0:rim] = send_ref[0:1, :].astype(F32)
     lists[0:1, rim : 2 * rim] = send_ref[1:2, :].astype(F32)
     columns[...] = lists[...].T
+    loads[7].wait()
     loads[1].wait()
-    loads[7].wait()
+    for i in (3, 2, 5, 9, 12, 6, 11, 0, 8, 10):
+        loads[i].start()
     known[0:owned, :] = (0.5 * dot(mesh_ref[...], w_src_ref[...])).astype(BF)
 
-    def select(side):
-        rows = pl.ds(pl.multiple_of(side * rim, rim), rim)
+    halves = (pl.ds(0, rim // 2), pl.ds(rim // 2, rim // 2))
+
+    def select(side, first, count):
+        rows = pl.ds(pl.multiple_of(side * rim + first, count), count)
         hot = one_hot_columns(columns[rows, 0:1].astype(jnp.int32), owned)
         return dot(hot, known[0:owned, :]).astype(BF)
 
     to_near = remote(
         out_halo.at[0], known.at[pl.ds(owned, rim)], halo_send.at[0], halo_recv.at[0], band=near_band
     )
-    to_far = remote(out_halo.at[1], away.at[pl.ds(0, rim)], halo_send.at[1], halo_recv.at[1], band=far_band)
-    out_halo[1] = select(far)
+    to_far = [
+        remote(
+            out_halo.at[1, rows], away.at[rows], halo_send.at[1 + i], halo_recv.at[1 + i], band=far_band
+        )
+        for i, rows in enumerate(halves)
+    ]
+    out_halo[1, halves[0], :] = select(far, 0, rim // 2)
     pl.semaphore_wait(
         barrier, n_member - 1 + jnp.where(has_below, 1, 0) + jnp.where(has_above, 1, 0)
     )
 
     @pl.when(has_far)
     def _():
-        to_far.start()
-
-    out_halo[0] = select(near)
+        to_far[0].start()
+
+    out_halo[1, halves[1], :] = select(far, rim // 2, rim // 2)
+
+    @pl.when(has_far)
+    def _():
+        to_far[1].start()
+
+    out_halo[0] = select(near, 0, rim)
     to_near.start()
 
     @pl.when(jnp.logical_not(has_far))
@@ -199,76 +220,69 @@
     w_out[0:fields, :] = w_out_ref[...]
     weights[...] = jnp.zeros_like(weights)
     weights[0:1, 0:fields] = weight_ref[...]
-    away[rim:, :] = jnp.zeros((LANES, channels), BF)
+    known[owned + rim :, :] = jnp.zeros((LANES, channels), BF)
     for feature in range(features):
         half = (0.5 * w_edge_ref[feature : feature + 1, :].astype(F32)).astype(BF)
         for edge in range(edges):
-            row = rim + COL_EDGE + feature * edges + edge
-            away[row : row + 1, :] = half
+            row = owned + rim + COL_EDGE + feature * edges + edge
+            known[row : row + 1, :] = half
     loads[0].wait()
     loads[8].wait()
     zhat[...] = 0.5 * dot(grid_ref[...], w_dst_ref[...])
     to_near.wait_recv()
 
     def gather_known(part):
-        rows = pl.ds(firsts[part], sizes[part])
-        hot = jnp.concatenate(
-            [
-                one_hot_columns(
-                    table[rows, COL_KNOWN + edge : COL_KNOWN + edge + 1].astype(jnp.int32), owned + rim
-                )
-                for edge in range(edges)
-            ],
-            axis=0,
-        )
-        found = dot(hot, known[...])
-        dst = zhat[rows, :]
-        for edge in range(edges):
-            base[edge, rows, :] = found[edge * sizes[part] : (edge + 1) * sizes[part], :] + dst
-
-    gather_known(0)
-    gather_known(1)
-    loads[10].wait()
-
-    @pl.when(has_far)
-    def _():
-        to_far.wait_recv()
-
-    gain = gain_ref[...]
-    reads = (read_even, read_odd)
-
-    def read(part):
         rows = pl.ds(firsts[part], sizes[part])
         lane = lax.broadcasted_iota(jnp.int32, (sizes[part], LANES), 1)
         values = table[rows, :]
         hots = []
         for edge in range(edges):
-            column = table[rows, COL_FAR + edge : COL_FAR + edge + 1].astype(jnp.int32)
+            column = table[rows, COL_KNOWN + edge : COL_KNOWN + edge + 1].astype(jnp.int32)
             chosen = (lane >= COL_EDGE) & (lane < COL_FAR) & (lax.rem(lane, edges) == edge)
             hots.append(
                 jnp.concatenate(
                     [
-                        one_hot_columns(column, rim),
+                        one_hot_columns(column, owned + rim),
                         jnp.where(chosen, values, 0.0).astype(BF),
                     ],
                     axis=1,
                 )
             )
-        reads[part % 2][0 : edges * sizes[part], :] = dot(jnp.concatenate(hots, axis=0), away[...])
+        found = dot(jnp.concatenate(hots, axis=0), known[...])
+        dst = zhat[rows, :]
+        for edge in range(edges):
+            base[edge, rows, :] = found[edge * sizes[part] : (edge + 1) * sizes[part], :] + dst
+
+    gather_known(0)
+    gather_known(1)
+    gather_known(2)
+    loads[10].wait()
+
+    @pl.when(has_far)
+    def _():
+        to_far[0].wait_recv()
+        to_far[1].wait_recv()
+
+    gain = gain_ref[...]
+    reads = (read_even, read_odd)
+
+    def read(part):
+        rows = pl.ds(firsts[part], sizes[part])
+        hots = [
+            one_hot_columns(table[rows, COL_FAR + edge : COL_FAR + edge + 1].astype(jnp.int32), rim)
+            for edge in range(edges)
+        ]
+        found = dot(jnp.concatenate(hots, axis=0), away[...])
+        reads[part % 2][0 : edges * sizes[part], :] = found
 
     def forward(part):
         rows = pl.ds(firsts[part], sizes[part])
         total = None
-        derivs = None
         for edge in range(edges):
             half = reads[part % 2][edge * sizes[part] : (edge + 1) * sizes[part], :] + base[edge, rows, :]
-            rise = jnp.tanh(half) + 1.0
-            act = half * rise
-            twice = rise + act * (2.0 - rise)
-            deriv[edge, rows, :] = twice.astype(BF)
+            base[edge, rows, :] = half
+            act = half * (jnp.tanh(half) + 1.0)
             total = act if total is None else total + act
-            derivs = twice if derivs is None else derivs + twice
-        deriv_sum[rows, :] = derivs
         z = grid_ref[rows, :].astype(F32) + dot(total.astype(BF), w_msg_ref[...])
         centre = z - jnp.mean(z, axis=1, keepdims=True)
         scale = lax.rsqrt(jnp.mean(centre * centre, axis=1, keepdims=True) + LN_EPS)
@@ -276,6 +290,17 @@
         zhat[rows, :] = hat
         rstd[rows, :] = jnp.broadcast_to(scale, (sizes[part], LANES))
         pred[rows, :] = dot_t((hat * gain).astype(BF), w_out[...]).astype(BF)
+
+    def derive(part):
+        rows = pl.ds(firsts[part], sizes[part])
+        total = None
+        for edge in range(edges):
+            half = base[edge, rows, :]
+            rise = jnp.tanh(half) + 1.0
+            twice = rise + half * rise * (2.0 - rise)
+            deriv[edge, rows, :] = twice.astype(BF)
+            total = twice if total is None else total + twice
+        deriv_sum[rows, :] = total
 
     def pred_copy(part, other):
         return remote(
@@ -351,8 +376,8 @@
         grads = jnp.concatenate([deriv[edge, rows, :] for edge in range(edges)], axis=0)
         return dot(one_hot_rows(names, height, first), grads)
 
-    def scatter_far(part):
-        return scatter(part, part, owned + far * rim, rim)
+    def scatter_far(part, first, count):
+        return scatter(part, part, owned + far * rim + first, count)
 
     read(0)
     forward(0)
@@ -360,59 +385,76 @@
     read(1)
     forward(1)
     send_pred(1)
-    compare(0)
-    gather_known(2)
     read(2)
     forward(2)
     send_pred(2)
+    compare(0)
+    derive(0)
     compare(1)
+    derive(1)
+    derive(2)
+    compare(2)
     backward(0)
-    rims[...] = scatter_far(0)
-    slots[...] = scatter(0, 0, 0, owned)
-    compare(2)
+    rims[...] = scatter_far(0, 0, rim)
     backward(1)
-    rims[...] += scatter_far(1)
-    slots[...] += scatter(1, 1, 0, owned)
+    rims[...] += scatter_far(1, 0, rim)
     backward(2)
-    d_halo[1] = (rims[...] + scatter_far(2)).astype(BF)
-
     back_near = remote(
         d_halo.at[0], back.at[pl.ds(0, rim)], back_send.at[0], back_recv.at[0], band=near_band
     )
-    back_far = remote(
-        d_halo.at[1], back.at[pl.ds(rim, rim)], back_send.at[1], back_recv.at[1], band=far_band
-    )
-
-    @pl.when(has_far)
-    def _():
-        back_far.start()
+    back_far = [
+        remote(
+            d_halo.at[1, rows],
+            back.at[pl.ds(rim + i * (rim // 2), rim // 2)],
+            back_send.at[1 + i],
+            back_recv.at[1 + i],
+            band=far_band,
+        )
+        for i, rows in enumerate(halves)
+    ]
+    d_halo[1, halves[0], :] = (rims[halves[0], :] + scatter_far(2, 0, rim // 2)).astype(BF)
+
+    @pl.when(has_far)
+    def _():
+        back_far[0].start()
+
+    d_halo[1, halves[1], :] = (rims[halves[1], :] + scatter_far(2, rim // 2, rim // 2)).astype(BF)
+
+    @pl.when(has_far)
+    def _():
+        back_far[1].start()
 
     d_halo[0] = scatter(0, 2, owned + near * rim, rim).astype(BF)
     back_near.start()
     d_grid[...] = (zhat[...] + dot_t(d_sum[...], w_dst_ref[...])).astype(BF)
-    slots[...] += scatter(2, 2, 0, owned)
-
-    def returned(side, place):
-        return dot(
-            one_hot_rows(send_ref[pl.ds(side, 1), :], owned, 0), back[place * rim : (place + 1) * rim, :]
-        )
+    slots[...] = scatter(0, 2, 0, owned)
+
+    def returned(side, first, place, count):
+        names = send_ref[pl.ds(side, 1), pl.ds(first, count)]
+        return dot(one_hot_rows(names, owned, 0), back[pl.ds(place, count), :])
 
     back_near.wait_recv()
-    slots[...] += returned(near, 0)
-
-    @pl.when(has_far)
-    def _():
-        back_far.wait_recv()
-
-    sums[...] = (slots[...] + returned(far, 1)).astype(BF)
+    slots[...] += returned(near, 0, 0, rim)
+
+    @pl.when(has_far)
+    def _():
+        back_far[0].wait_recv()
+
+    slots[...] += returned(far, 0, rim, rim // 2)
+
+    @pl.when(has_far)
+    def _():
+        back_far[1].wait_recv()
+
+    sums[...] = (slots[...] + returned(far, rim // 2, rim + rim // 2, rim // 2)).astype(BF)
 
     to_near.wait_send()
     back_near.wait_send()
 
     @pl.when(has_far)
     def _():
-        to_far.wait_send()
-        back_far.wait_send()
+        for copy in to_far + back_far:
+            copy.wait_send()
 
     all_of((n_member - 1) * sum(shares), pred_send, pred_recv.at[0]).wait_send()
     all_of((n_member - 1) * sum(shares), d_send, d_recv.at[0]).wait_send()
@@ -494,9 +536,9 @@
             pltpu.VMEM((LANES, channels), BF),
             pltpu.VMEM((1, LANES), F32),
             pltpu.VMEM((2 * rim, 8), F32),
-            pltpu.VMEM((owned + rim, channels), BF),
+            pltpu.VMEM((owned + rim + LANES, channels), BF),
             pltpu.VMEM((2, rim, channels), BF),
-            pltpu.VMEM((rim + LANES, channels), BF),
+            pltpu.VMEM((rim, channels), BF),
             pltpu.VMEM((edges, points, channels), F32),
             pltpu.VMEM((edges * largest, channels), F32),
             pltpu.VMEM((edges * largest, channels), F32),
@@ -514,14 +556,14 @@
             pltpu.VMEM((2, rim, channels), BF),
             pltpu.VMEM((2 * rim, channels), BF),
             dma((len(operands),)),
-            dma((2,)),
-            dma((2,)),
+            dma((3,)),
+            dma((3,)),
             dma,
             dma((len(PARTS),)),
             dma,
             dma((len(PARTS),)),
-            dma((2,)),
-            dma((2,)),
+            dma((3,)),
+            dma((3,)),
         ],
         compiler_params=pltpu.CompilerParams(
             collective_id=0, has_side_effects=True, vmem_limit_bytes=52 * 2**20

time: 48.9 us -> 45.6 us (0.933)
  Pallas kernels: 48 us -> 44.7 us
    pallas_call x1, Pallas kernels: 46.3 us -> 42.9 us  [per_device(): pl.pallas_call(functools.partial(kernel, n_band, n_member), out_shape=(pl...]
where the time goes in v4:
time: 45.6 us; the launch traced here: 45.5 us
  Pallas kernels  44.7 us (98%)
  between operations  0.82 us (2%)
    pallas_call x1, Pallas kernels, per_device(): pl.pallas_call(functools.partial(kernel, n_band, n_member), out_shape=(pl...  42.9 us
    pallas_call x1, Pallas kernels, per_device(): pl.pallas_call(finish, out_shape=(jax.ShapeDtypeStruct((points, channels)...  1.74 us

profile of v4, /device:TPU:24, one launch (start us, length us, event | category | flops | bytes accessed | tf_op | source)
XLA Modules:
  0.0 45.5 jit_solution(16737950923287927018)
XLA Ops:
  0.6 0.0 copy-start
  0.6 42.9 %shard_map.140 = (bf16[1024,512]{1,0:T(8,128)(2,1)S(1)}, bf16[1024,512]{1,0:T(8,128)(2,1)S(1)}) custom-call(bf16[1024,512]{1,0:T(8,128)(2,1)} %bitcast.8, bf16[1024,512]{1,0:T(8,128)(2,1)} %bitcast.9, bf16[4,4,1024]{2,1,0:T(4,128)(2,1)} %refs_2_.1, s32[4,1024]{1,0:T(4,128)} %bitcast.11, s32[2,512]{1,0:T(2,128)} %refs_4_.1, f32[100,1024]{1,0:T(8,128)} %refs_5_.1, ...), custom_call_target="tpu_custom_call" | custom-call | tf_op jit(solution)/shard_map/pallas_call | solution.py:526
  43.6 0.0 copy-done
  43.6 1.7 %shard_map.141 = (bf16[1024,512]{1,0:T(8,128)(2,1)}, bf16[1024,512]{1,0:T(8,128)(2,1)}) custom-call(bf16[1024,512]{1,0:T(8,128)(2,1)S(1)} %get-tuple-element.6.d_grid, bf16[1024,512]{1,0:T(8,128)(2,1)S(1)} %get-tuple-element.7.sums, bf16[512,512]{1,0:T(8,128)(2,1)S(1)} %copy-done), custom_call_target="tpu_custom_call" | custom-call | tf_op jit(solution)/shard_map/pallas_call | solution.py:572
Async XLA Ops:
  0.6 43.0 %copy-start = (bf16[512,512]{1,0:T(8,128)(2,1)S(1)}, bf16[512,512]{1,0:T(8,128)(2,1)}, u32[]{:S(2)}) copy-start(bf16[512,512]{1,0:T(8,128)(2,1)} %w_src.1) | copy-start | bytes 1572868

commit v5 on v4

--- a/solution.py
+++ b/solution.py
@@ -82,8 +82,6 @@
         out_halo,
         away,
         base,
-        read_even,
-        read_odd,
         deriv,
         deriv_sum,
         zhat,
@@ -151,7 +149,7 @@
         pl.semaphore_signal(barrier, inc=1, device_id={"member": other}, device_id_type=MESH_ID)
 
     loads = [pltpu.make_async_copy(hbm[i], held[i], load_sem.at[i]) for i in range(13)]
-    for i in (4, 7, 1):
+    for i in (4, 1, 7):
         loads[i].start()
 
     loads[4].wait()
@@ -159,18 +157,15 @@
     lists[0:1, 0:rim] = send_ref[0:1, :].astype(F32)
     lists[0:1, rim : 2 * rim] = send_ref[1:2, :].astype(F32)
     columns[...] = lists[...].T
-    loads[7].wait()
-    loads[1].wait()
-    for i in (3, 2, 5, 9, 12, 6, 11, 0, 8, 10):
-        loads[i].start()
-    known[0:owned, :] = (0.5 * dot(mesh_ref[...], w_src_ref[...])).astype(BF)
-
     halves = (pl.ds(0, rim // 2), pl.ds(rim // 2, rim // 2))
 
-    def select(side, first, count):
+    def project(rows):
+        return (0.5 * dot(rows, w_src_ref[...])).astype(BF)
+
+    def select(source, side, first, count):
         rows = pl.ds(pl.multiple_of(side * rim + first, count), count)
         hot = one_hot_columns(columns[rows, 0:1].astype(jnp.int32), owned)
-        return dot(hot, known[0:owned, :]).astype(BF)
+        return dot(hot, source[0:owned, :]).astype(BF)
 
     to_near = remote(
         out_halo.at[0], known.at[pl.ds(owned, rim)], halo_send.at[0], halo_recv.at[0], band=near_band
@@ -181,7 +176,12 @@
         )
         for i, rows in enumerate(halves)
     ]
-    out_halo[1, halves[0], :] = select(far, 0, rim // 2)
+    loads[1].wait()
+    picked = select(mesh_ref, far, 0, rim // 2)
+    loads[7].wait()
+    for i in (3, 2, 5, 9, 12, 6, 11, 0, 8, 10):
+        loads[i].start()
+    out_halo[1, halves[0], :] = project(picked)
     pl.semaphore_wait(
         barrier, n_member - 1 + jnp.where(has_below, 1, 0) + jnp.where(has_above, 1, 0)
     )
@@ -190,13 +190,14 @@
     def _():
         to_far[0].start()
 
-    out_halo[1, halves[1], :] = select(far, rim // 2, rim // 2)
+    out_halo[1, halves[1], :] = project(select(mesh_ref, far, rim // 2, rim // 2))
 
     @pl.when(has_far)
     def _():
         to_far[1].start()
 
-    out_halo[0] = select(near, 0, rim)
+    known[0:owned, :] = project(mesh_ref[...])
+    out_halo[0] = select(known, near, 0, rim)
     to_near.start()
 
     @pl.when(jnp.logical_not(has_far))
@@ -258,28 +259,38 @@
     gather_known(2)
     loads[10].wait()
 
-    @pl.when(has_far)
-    def _():
-        to_far[0].wait_recv()
-        to_far[1].wait_recv()
-
     gain = gain_ref[...]
-    reads = (read_even, read_odd)
-
-    def read(part):
+    def read(part, side):
         rows = pl.ds(firsts[part], sizes[part])
         hots = [
-            one_hot_columns(table[rows, COL_FAR + edge : COL_FAR + edge + 1].astype(jnp.int32), rim)
+            one_hot_columns(
+                table[rows, COL_FAR + edge : COL_FAR + edge + 1].astype(jnp.int32) - side * (rim // 2),
+                rim // 2,
+            )
             for edge in range(edges)
         ]
-        found = dot(jnp.concatenate(hots, axis=0), away[...])
-        reads[part % 2][0 : edges * sizes[part], :] = found
+        return dot(jnp.concatenate(hots, axis=0), away[halves[side], :])
+
+    @pl.when(has_far)
+    def _():
+        to_far[0].wait_recv()
+
+    for part in range(len(PARTS)):
+        rows = pl.ds(firsts[part], sizes[part])
+        found = read(part, 0)
+        for edge in range(edges):
+            base[edge, rows, :] += found[edge * sizes[part] : (edge + 1) * sizes[part], :]
+
+    @pl.when(has_far)
+    def _():
+        to_far[1].wait_recv()
 
     def forward(part):
         rows = pl.ds(firsts[part], sizes[part])
+        found = read(part, 1)
         total = None
         for edge in range(edges):
-            half = reads[part % 2][edge * sizes[part] : (edge + 1) * sizes[part], :] + base[edge, rows, :]
+            half = found[edge * sizes[part] : (edge + 1) * sizes[part], :] + base[edge, rows, :]
             base[edge, rows, :] = half
             act = half * (jnp.tanh(half) + 1.0)
             total = act if total is None else total + act
@@ -295,11 +306,11 @@
         rows = pl.ds(firsts[part], sizes[part])
         total = None
         for edge in range(edges):
-            half = base[edge, rows, :]
+            half = base[edge, rows, :].astype(BF)
             rise = jnp.tanh(half) + 1.0
             twice = rise + half * rise * (2.0 - rise)
-            deriv[edge, rows, :] = twice.astype(BF)
-            total = twice if total is None else total + twice
+            deriv[edge, rows, :] = twice
+            total = twice.astype(F32) if total is None else total + twice.astype(F32)
         deriv_sum[rows, :] = total
 
     def pred_copy(part, other):
@@ -379,19 +390,16 @@
     def scatter_far(part, first, count):
         return scatter(part, part, owned + far * rim + first, count)
 
-    read(0)
     forward(0)
     send_pred(0)
-    read(1)
     forward(1)
     send_pred(1)
-    read(2)
     forward(2)
     send_pred(2)
     compare(0)
     derive(0)
+    derive(1)
     compare(1)
-    derive(1)
     derive(2)
     compare(2)
     backward(0)
@@ -502,7 +510,6 @@
     rim = send_rows.shape[1]
     fields = target.shape[0]
     share = points // n_member
-    largest = max(PARTS) * UNIT
     operands = (
         grid_rows,
         mesh_rows,
@@ -540,8 +547,6 @@
             pltpu.VMEM((2, rim, channels), BF),
             pltpu.VMEM((rim, channels), BF),
             pltpu.VMEM((edges, points, channels), F32),
-            pltpu.VMEM((edges * largest, channels), F32),
-            pltpu.VMEM((edges * largest, channels), F32),
             pltpu.VMEM((edges, points, channels), BF),
             wide_latents,
             wide_latents,

time: 45.6 us -> 46.3 us (1.015)
  Pallas kernels: 44.7 us -> 45.4 us
    pallas_call x1, Pallas kernels: 42.9 us -> 43.6 us  [per_device(): pl.pallas_call(functools.partial(kernel, n_band, n_member), out_shape=(pl...]
where the time goes in v5:
time: 46.3 us; the launch traced here: 46.2 us
  Pallas kernels  45.4 us (98%)
  between operations  0.82 us (2%)
    pallas_call x1, Pallas kernels, per_device(): pl.pallas_call(functools.partial(kernel, n_band, n_member), out_shape=(pl...  43.6 us
    pallas_call x1, Pallas kernels, per_device(): pl.pallas_call(finish, out_shape=(jax.ShapeDtypeStruct((points, channels)...  1.74 us

profile of v5, /device:TPU:24, one launch (start us, length us, event | category | flops | bytes accessed | tf_op | source)
XLA Modules:
  0.0 46.2 jit_solution(7585034647202415571)
XLA Ops:
  0.6 0.0 copy-start
  0.6 43.6 %shard_map.140 = (bf16[1024,512]{1,0:T(8,128)(2,1)S(1)}, bf16[1024,512]{1,0:T(8,128)(2,1)S(1)}) custom-call(bf16[1024,512]{1,0:T(8,128)(2,1)} %bitcast.8, bf16[1024,512]{1,0:T(8,128)(2,1)} %bitcast.9, bf16[4,4,1024]{2,1,0:T(4,128)(2,1)} %refs_2_.1, s32[4,1024]{1,0:T(4,128)} %bitcast.11, s32[2,512]{1,0:T(2,128)} %refs_4_.1, f32[100,1024]{1,0:T(8,128)} %refs_5_.1, ...), custom_call_target="tpu_custom_call" | custom-call | tf_op jit(solution)/shard_map/pallas_call | solution.py:533
  44.3 0.0 copy-done
  44.3 1.7 %shard_map.141 = (bf16[1024,512]{1,0:T(8,128)(2,1)}, bf16[1024,512]{1,0:T(8,128)(2,1)}) custom-call(bf16[1024,512]{1,0:T(8,128)(2,1)S(1)} %get-tuple-element.6.d_grid, bf16[1024,512]{1,0:T(8,128)(2,1)S(1)} %get-tuple-element.7.sums, bf16[512,512]{1,0:T(8,128)(2,1)S(1)} %copy-done), custom_call_target="tpu_custom_call" | custom-call | tf_op jit(solution)/shard_map/pallas_call | solution.py:577
Async XLA Ops:
  0.6 43.6 %copy-start = (bf16[512,512]{1,0:T(8,128)(2,1)S(1)}, bf16[512,512]{1,0:T(8,128)(2,1)}, u32[]{:S(2)}) copy-start(bf16[512,512]{1,0:T(8,128)(2,1)} %w_src.1) | copy-start | bytes 1572868

commit v6 on v4

--- a/solution.py
+++ b/solution.py
@@ -82,19 +82,14 @@
         out_halo,
         away,
         base,
-        read_even,
-        read_odd,
+        found_far,
         deriv,
-        deriv_sum,
         zhat,
         rstd,
         pred,
         peers,
         d_peers,
         d_pred,
-        d_sum,
-        slots,
-        rims,
         d_halo,
         back,
         load_sem,
@@ -264,7 +259,6 @@
         to_far[1].wait_recv()
 
     gain = gain_ref[...]
-    reads = (read_even, read_odd)
 
     def read(part):
         rows = pl.ds(firsts[part], sizes[part])
@@ -273,13 +267,13 @@
             for edge in range(edges)
         ]
         found = dot(jnp.concatenate(hots, axis=0), away[...])
-        reads[part % 2][0 : edges * sizes[part], :] = found
+        found_far[0 : edges * sizes[part], :] = found
 
     def forward(part):
         rows = pl.ds(firsts[part], sizes[part])
         total = None
         for edge in range(edges):
-            half = reads[part % 2][edge * sizes[part] : (edge + 1) * sizes[part], :] + base[edge, rows, :]
+            half = found_far[edge * sizes[part] : (edge + 1) * sizes[part], :] + base[edge, rows, :]
             base[edge, rows, :] = half
             act = half * (jnp.tanh(half) + 1.0)
             total = act if total is None else total + act
@@ -293,14 +287,11 @@
 
     def derive(part):
         rows = pl.ds(firsts[part], sizes[part])
-        total = None
         for edge in range(edges):
-            half = base[edge, rows, :]
+            half = base[edge, rows, :].astype(BF)
             rise = jnp.tanh(half) + 1.0
             twice = rise + half * rise * (2.0 - rise)
-            deriv[edge, rows, :] = twice.astype(BF)
-            total = twice if total is None else total + twice
-        deriv_sum[rows, :] = total
+            deriv[edge, rows, :] = twice
 
     def pred_copy(part, other):
         return remote(
@@ -364,9 +355,7 @@
             - hat * jnp.mean(scaled * hat, axis=1, keepdims=True)
         )
         zhat[rows, :] = d_z
-        d_act = 0.5 * dot_t(d_z.astype(BF), w_msg_ref[...])
-        d_sum[rows, :] = (d_act * deriv_sum[rows, :]).astype(BF)
-        d_act = d_act.astype(BF)
+        d_act = (0.5 * dot_t(d_z.astype(BF), w_msg_ref[...])).astype(BF)
         for edge in range(edges):
             deriv[edge, rows, :] = d_act * deriv[edge, rows, :]
 
@@ -375,6 +364,8 @@
         names = jnp.concatenate([near_ref[edge : edge + 1, rows] for edge in range(edges)], axis=1)
         grads = jnp.concatenate([deriv[edge, rows, :] for edge in range(edges)], axis=0)
         return dot(one_hot_rows(names, height, first), grads)
+
+    slots, rims = base.at[0], base.at[1, pl.ds(0, rim)]
 
     def scatter_far(part, first, count):
         return scatter(part, part, owned + far * rim + first, count)
@@ -426,7 +417,10 @@
 
     d_halo[0] = scatter(0, 2, owned + near * rim, rim).astype(BF)
     back_near.start()
-    d_grid[...] = (zhat[...] + dot_t(d_sum[...], w_dst_ref[...])).astype(BF)
+    d_sum = deriv[0].astype(F32)
+    for edge in range(1, edges):
+        d_sum = d_sum + deriv[edge].astype(F32)
+    d_grid[...] = (zhat[...] + dot_t(d_sum.astype(BF), w_dst_ref[...])).astype(BF)
     slots[...] = scatter(0, 2, 0, owned)
 
     def returned(side, first, place, count):
@@ -463,9 +457,9 @@
 def finish(d_grid, sums, w_src, grid_out, mesh_out, rows_out, store_sem):
     through = pltpu.make_async_copy(d_grid, grid_out, store_sem.at[0])
     through.start()
-    height = sums.shape[0] // 2
+    height = sums.shape[0] // 4
     stores = []
-    for part in range(2):
+    for part in range(4):
         rows = pl.ds(part * height, height)
         rows_out[rows, :] = dot_t(sums[rows, :], w_src[...]).astype(BF)
         stores.append(
@@ -541,18 +535,13 @@
             pltpu.VMEM((rim, channels), BF),
             pltpu.VMEM((edges, points, channels), F32),
             pltpu.VMEM((edges * largest, channels), F32),
-            pltpu.VMEM((edges * largest, channels), F32),
             pltpu.VMEM((edges, points, channels), BF),
-            wide_latents,
             wide_latents,
             pltpu.VMEM((points, LANES), F32),
             pltpu.VMEM((points, LANES), BF),
             pltpu.VMEM((n_member, share, LANES), BF),
             pltpu.VMEM((n_member, share, LANES), BF),
             pltpu.VMEM((points, LANES), BF),
-            latents,
-            wide_latents,
-            pltpu.VMEM((rim, channels), F32),
             pltpu.VMEM((2, rim, channels), BF),
             pltpu.VMEM((2 * rim, channels), BF),
             dma((len(operands),)),
@@ -577,7 +566,7 @@
         ),
         in_specs=[vmem] * 3,
         out_specs=(anywhere, anywhere),
-        scratch_shapes=[latents, dma((3,))],
+        scratch_shapes=[latents, dma((5,))],
         compiler_params=pltpu.CompilerParams(vmem_limit_bytes=16 * 2**20),
     )(d_grid, sums, w_src)
     return d_grid[None], d_mesh[None]

time: 45.6 us -> 45.3 us (level)
  no operation moved by 1% of the time
where the time goes in v6:
time: 45.3 us; the launch traced here: 45.2 us
  Pallas kernels  44.4 us (98%)
  between operations  0.82 us (2%)
    pallas_call x1, Pallas kernels, per_device(): pl.pallas_call(functools.partial(kernel, n_band, n_member), out_shape=(pl...  42.9 us
    pallas_call x1, Pallas kernels, per_device(): pl.pallas_call(finish, out_shape=(jax.ShapeDtypeStruct((points, channels)...  1.49 us

profile of v6, /device:TPU:24, one launch (start us, length us, event | category | flops | bytes accessed | tf_op | source)
XLA Modules:
  0.0 45.2 jit_solution(4868051357542643765)
XLA Ops:
  0.6 0.0 copy-start
  0.6 42.9 %shard_map.140 = (bf16[1024,512]{1,0:T(8,128)(2,1)S(1)}, bf16[1024,512]{1,0:T(8,128)(2,1)S(1)}) custom-call(bf16[1024,512]{1,0:T(8,128)(2,1)} %bitcast.8, bf16[1024,512]{1,0:T(8,128)(2,1)} %bitcast.9, bf16[4,4,1024]{2,1,0:T(4,128)(2,1)} %refs_2_.1, s32[4,1024]{1,0:T(4,128)} %bitcast.11, s32[2,512]{1,0:T(2,128)} %refs_4_.1, f32[100,1024]{1,0:T(8,128)} %refs_5_.1, ...), custom_call_target="tpu_custom_call" | custom-call | tf_op jit(solution)/shard_map/pallas_call | solution.py:520
  43.5 0.0 copy-done
  43.5 1.5 %shard_map.141 = (bf16[1024,512]{1,0:T(8,128)(2,1)}, bf16[1024,512]{1,0:T(8,128)(2,1)}) custom-call(bf16[1024,512]{1,0:T(8,128)(2,1)S(1)} %get-tuple-element.6.d_grid, bf16[1024,512]{1,0:T(8,128)(2,1)S(1)} %get-tuple-element.7.sums, bf16[512,512]{1,0:T(8,128)(2,1)S(1)} %copy-done), custom_call_target="tpu_custom_call" | custom-call | tf_op jit(solution)/shard_map/pallas_call | solution.py:561
Async XLA Ops:
  0.6 42.9 %copy-start = (bf16[512,512]{1,0:T(8,128)(2,1)S(1)}, bf16[512,512]{1,0:T(8,128)(2,1)}, u32[]{:S(2)}) copy-start(bf16[512,512]{1,0:T(8,128)(2,1)} %w_src.1) | copy-start | bytes 1572868

commit v7 on v6

--- a/solution.py
+++ b/solution.py
@@ -185,14 +185,13 @@
     def _():
         to_far[0].start()
 
-    out_halo[1, halves[1], :] = select(far, rim // 2, rim // 2)
-
-    @pl.when(has_far)
-    def _():
-        to_far[1].start()
-
     out_halo[0] = select(near, 0, rim)
     to_near.start()
+    out_halo[1, halves[1], :] = select(far, rim // 2, rim // 2)
+
+    @pl.when(has_far)
+    def _():
+        to_far[1].start()
 
     @pl.when(jnp.logical_not(has_far))
     def _():

time: 45.3 us -> 44.6 us (0.985)
  Pallas kernels: 44.4 us -> 43.7 us
    pallas_call x1, Pallas kernels: 42.9 us -> 42.2 us  [per_device(): pl.pallas_call(functools.partial(kernel, n_band, n_member), out_shape=(pl...]
where the time goes in v7:
time: 44.6 us; the launch traced here: 44.5 us
  Pallas kernels  43.7 us (98%)
  between operations  0.82 us (2%)
    pallas_call x1, Pallas kernels, per_device(): pl.pallas_call(functools.partial(kernel, n_band, n_member), out_shape=(pl...  42.2 us
    pallas_call x1, Pallas kernels, per_device(): pl.pallas_call(finish, out_shape=(jax.ShapeDtypeStruct((points, channels)...  1.49 us

profile of v7, /device:TPU:24, one launch (start us, length us, event | category | flops | bytes accessed | tf_op | source)
XLA Modules:
  0.0 44.5 jit_solution(2416588932098478549)
XLA Ops:
  0.6 0.0 copy-start
  0.6 42.2 %shard_map.140 = (bf16[1024,512]{1,0:T(8,128)(2,1)S(1)}, bf16[1024,512]{1,0:T(8,128)(2,1)S(1)}) custom-call(bf16[1024,512]{1,0:T(8,128)(2,1)} %bitcast.8, bf16[1024,512]{1,0:T(8,128)(2,1)} %bitcast.9, bf16[4,4,1024]{2,1,0:T(4,128)(2,1)} %refs_2_.1, s32[4,1024]{1,0:T(4,128)} %bitcast.11, s32[2,512]{1,0:T(2,128)} %refs_4_.1, f32[100,1024]{1,0:T(8,128)} %refs_5_.1, ...), custom_call_target="tpu_custom_call" | custom-call | tf_op jit(solution)/shard_map/pallas_call | solution.py:519
  42.8 0.0 copy-done
  42.8 1.5 %shard_map.141 = (bf16[1024,512]{1,0:T(8,128)(2,1)}, bf16[1024,512]{1,0:T(8,128)(2,1)}) custom-call(bf16[1024,512]{1,0:T(8,128)(2,1)S(1)} %get-tuple-element.6.d_grid, bf16[1024,512]{1,0:T(8,128)(2,1)S(1)} %get-tuple-element.7.sums, bf16[512,512]{1,0:T(8,128)(2,1)S(1)} %copy-done), custom_call_target="tpu_custom_call" | custom-call | tf_op jit(solution)/shard_map/pallas_call | solution.py:560
Async XLA Ops:
  0.6 42.2 %copy-start = (bf16[512,512]{1,0:T(8,128)(2,1)S(1)}, bf16[512,512]{1,0:T(8,128)(2,1)}, u32[]{:S(2)}) copy-start(bf16[512,512]{1,0:T(8,128)(2,1)} %w_src.1) | copy-start | bytes 1572868
